TPU v7x, 32 devices: a whole 2x2x4 slice. The times are simulated.
32 devices in a mesh: dp: 4 (over y, x), ctx: 4 (over z), head: 2 (over core).
Axes of the slice: x: 2, y: 2, z: 4, core: 2. Of those that a mesh axis runs over, the one named last changes fastest.
Arguments:
- tokens: bfloat16 [8, 1024, 1024], P('dp', 'ctx'), may hold values from -6 to 6
- segments: int32 [8, 1024], P('dp', 'ctx'), may hold values from 0 to 5, as said below
- cotangent: bfloat16 [8, 1024, 1024], P('dp', 'ctx'), may hold values from -6 to 6
- inner_proj: bfloat16 [2, 1024, 2, 2048], P(None, ('dp', 'ctx'), None, 'head'), may hold values from -0.1875 to 0.1875
- state_proj: bfloat16 [2, 1024, 256], P(None, ('dp', 'ctx')), may hold values from -0.1875 to 0.1875
- step_proj: bfloat16 [2, 1024, 32], P(None, ('dp', 'ctx'), 'head'), may hold values from -0.1875 to 0.1875
- out_proj: bfloat16 [2, 2048, 1024], P(None, 'head', ('dp', 'ctx')), may hold values from -0.125 to 0.125
- norm_gain: float32 [2, 1024], replicated, may hold values from 0.5 to 1.5
- mix_kernel: float32 [2, 4, 2048], P(None, None, 'head'), may hold values from -3 to 3
- mix_bias: float32 [2, 2048], P(None, 'head'), may hold values from -3 to 3
- state_kernel: float32 [2, 4, 256], replicated, may hold values from -3 to 3
- state_bias: float32 [2, 256], replicated, may hold values from -3 to 3
- step_bias: float32 [2, 32], P(None, 'head'), may hold values from -4 to -2
- decay_log: float32 [2, 32], P(None, 'head'), may hold values from -12 to 1
- skip_gain: float32 [2, 32], P(None, 'head'), may hold values from 0.5 to 1.5
- gate_gain: float32 [2, 2048], P(None, 'head'), may hold values from 0.5 to 1.5
Outputs:
- mixed: bfloat16 [8, 1024, 1024], P('dp', 'ctx')
- token_grad: bfloat16 [8, 1024, 1024], P('dp', 'ctx')
- grad_inner_proj: float32 [2, 1024, 2, 2048], P(None, ('dp', 'ctx'), None, 'head')
- grad_state_proj: float32 [2, 1024, 256], P(None, ('dp', 'ctx'))
- grad_step_proj: float32 [2, 1024, 32], P(None, ('dp', 'ctx'), 'head')
- grad_out_proj: float32 [2, 2048, 1024], P(None, 'head', ('dp', 'ctx'))
- grad_norm_gain: float32 [2, 1024], replicated
- grad_mix_kernel: float32 [2, 4, 2048], P(None, None, 'head')
- grad_mix_bias: float32 [2, 2048], P(None, 'head')
- grad_state_kernel: float32 [2, 4, 256], replicated
- grad_state_bias: float32 [2, 256], replicated
- grad_step_bias: float32 [2, 32], P(None, 'head')
- grad_decay_log: float32 [2, 32], P(None, 'head')
- grad_skip_gain: float32 [2, 32], P(None, 'head')
- grad_gate_gain: float32 [2, 2048], P(None, 'head')
Inputs may be any that keep to these rules, and one draw needn't show every extreme that they name: `segments`: in each sequence the numbers start at 0 and rise by one where a document begins; a document has 200 to 2000 tokens, except the last of a sequence, which may be shorter, and except a document that makes up a whole sequence, which has all of its tokens; in each group of 2 consecutive sequences at least one is a single document.
All inputs are finite; a program needn't handle non-finite values.
Results may differ from a plain program's by a relative error of at most 0.02.
Values may be sent and summed in bfloat16 or wider, within the bound.
No kernel may reach another device: no remote copies, remote signals or barrier semaphores. Data moves between devices by JAX's collectives and lax.ppermute only.
A program may use at most 256 MiB of HBM per device.

v0:
```python
from functools import partial

import jax
import jax.numpy as jnp
from jax import lax
from jax.sharding import PartitionSpec as P

DI = 2048


EPSILON = 1e-05
HIGH = lax.Precision.HIGHEST


def from_behind(x, axis, by):
    size = lax.axis_size(axis)
    pairs = [(i, i + by) for i in range(size) if 0 <= i + by < size]
    return lax.ppermute(x, axis, pairs)


def entering(value, axis, join, neutral, backward):
    count, mine = (lax.axis_size(axis), lax.axis_index(axis))
    pieces = jax.tree.map(lambda part: lax.all_gather(part, axis), value)
    if backward:
        pieces = jax.tree.map(lambda part: part[::-1], pieces)
        mine = count - 1 - mine
    running = jax.tree.map(
        lambda part, zero: jnp.full_like(part, 0) + jnp.asarray(zero, part.dtype), value, neutral
    )

    def turn(position, running):
        longer = join(running, jax.tree.map(lambda part: part[position], pieces))
        return jax.tree.map(lambda new, old: jnp.where(position < mine, new, old), longer, running)

    return lax.fori_loop(0, count - 1, turn, running)


def scaled_norm(residual, gain):
    return (
        residual * lax.rsqrt(jnp.mean(residual * residual, axis=-1, keepdims=True) + EPSILON) * gain
    )


def conv_act(window, weight, bias, labels, segment):
    count = segment.shape[-1]
    total = bias
    for offset in range(weight.shape[0]):
        match = (labels[..., offset : offset + count] == segment).astype(jnp.float32)[..., None]
        total = total + weight[offset] * window[..., offset : offset + count, :] * match
    return jax.nn.silu(total)


def block_local(inner, bstate, cstate, steps_raw, step_bias, decay_log, skip_gain, segment, before):
    count = segment.shape[0]
    delta = jax.nn.softplus(steps_raw + step_bias)
    accrued = jnp.cumsum(-delta * jnp.exp(decay_log), axis=0)
    order = jnp.arange(count)
    same = (segment[:, None] == segment[None, :]) & (order[:, None] >= order[None, :])
    within = jnp.where(same[:, :, None], accrued[:, None, :] - accrued[None, :, :], 0.0)
    decay = jnp.exp(within) * same.astype(jnp.float32)[:, :, None]
    gram = jnp.dot(cstate, bstate.T, precision=HIGH)
    scaled = inner * delta[:, :, None]
    output = (
        jnp.einsum("tsh,shp->thp", gram[:, :, None] * decay, scaled, precision=HIGH)
        + skip_gain[None, :, None] * inner
    )
    entry = jnp.exp(accrued) * (segment == before).astype(jnp.float32)[:, None]
    tail = (
        jnp.exp(accrued[-1][None, :] - accrued)
        * (segment == segment[-1]).astype(jnp.float32)[:, None]
    )
    local = jnp.einsum("sh,shp,sn->hpn", tail, scaled, bstate, precision=HIGH)
    carry = jnp.exp(accrued[-1]) * (segment[-1] == before).astype(jnp.float32)
    return (output, entry, local, carry)


def local_mixer(inner, bstate, cstate, steps_raw, step_bias, decay_log, skip_gain, segment, before):

    def single(item):
        return block_local(
            item[0], item[1], item[2], item[3], step_bias, decay_log, skip_gain, item[4], item[5]
        )

    return lax.map(jax.checkpoint(single), (inner, bstate, cstate, steps_raw, segment, before))


def chain(earlier, later):
    return (earlier[0] * later[0], later[0][..., None, None] * earlier[1] + later[1])


def gated_out(output, entry, cstate, carried, gate):
    reach = jnp.einsum("stn,shpn->sthp", cstate, carried, precision=HIGH)
    mixer = output + entry[..., None] * reach
    return mixer.reshape(mixer.shape[0], mixer.shape[1], -1) * jax.nn.silu(gate)


def gate_norm(gated, total, gain):
    return gated * lax.rsqrt(total / DI + EPSILON)[..., None] * gain


def layer_forward(residual, segment, labels, full, small):
    inner_proj, state_proj, step_proj, out_proj = full
    (
        norm_gain,
        mix_kernel,
        mix_bias,
        state_kernel,
        state_bias,
        step_bias,
        decay_log,
        skip_gain,
        gate_gain,
    ) = small
    batch, count = segment.shape
    taps = mix_kernel.shape[0]
    heads = step_proj.shape[1]
    width = inner_proj.shape[2]
    states = state_proj.shape[1] // 2
    normed = scaled_norm(residual, norm_gain).astype(jnp.bfloat16)
    both = jnp.einsum("scd,dkq->sckq", normed, inner_proj, preferred_element_type=jnp.float32)
    gate = both[:, :, 0]
    inner_raw = both[:, :, 1].astype(jnp.bfloat16)
    state_raw = jnp.einsum(
        "scd,dn->scn", normed, state_proj, preferred_element_type=jnp.float32
    ).astype(jnp.bfloat16)
    steps_wide = jnp.einsum("scd,dh->sch", normed, step_proj, preferred_element_type=jnp.float32)
    stack = jnp.concatenate([inner_raw, state_raw], axis=2)
    rim = from_behind(stack[:, count - taps + 1 :], "ctx", 1)
    window = jnp.concatenate([rim, stack], axis=1).astype(jnp.float32)
    weight = jnp.concatenate([mix_kernel, state_kernel], axis=1)
    bias = jnp.concatenate([mix_bias, state_bias])
    active = conv_act(window, weight, bias, labels, segment).astype(jnp.bfloat16)
    inner = active[..., :width].astype(jnp.float32).reshape(batch, count, heads, width // heads)
    bstate = active[..., width : width + states].astype(jnp.float32)
    cstate = active[..., width + states :].astype(jnp.float32)
    before = labels[:, taps - 2]
    output, entry, local, carry = local_mixer(
        inner, bstate, cstate, steps_wide, step_bias, decay_log, skip_gain, segment, before
    )
    carried = entering(
        (carry, local), "ctx", chain, (jnp.ones_like(carry), jnp.zeros_like(local)), False
    )[1]
    gated = gated_out(output, entry, cstate, carried, gate)
    total = lax.psum(jnp.sum(gated * gated, axis=-1), "head")
    normal = gate_norm(gated, total, gate_gain).astype(jnp.bfloat16)
    part = jnp.einsum("scq,qd->scd", normal, out_proj, preferred_element_type=jnp.float32)
    branch = lax.psum(part, "head")
    kept = (
        residual,
        normed,
        gate,
        steps_wide,
        window,
        inner,
        bstate,
        cstate,
        output,
        entry,
        carry,
        carried,
        gated,
        total,
        normal,
        weight,
        bias,
        before,
    )
    return (residual + branch, kept)


def layer_backward(upstream, segment, labels, full, small, kept):
    inner_proj, state_proj, step_proj, out_proj = full
    (
        norm_gain,
        mix_kernel,
        mix_bias,
        state_kernel,
        state_bias,
        step_bias,
        decay_log,
        skip_gain,
        gate_gain,
    ) = small
    (
        residual,
        normed,
        gate,
        steps_wide,
        window,
        inner,
        bstate,
        cstate,
        output,
        entry,
        carry,
        carried,
        gated,
        total,
        normal,
        weight,
        bias,
        before,
    ) = kept
    batch, count = segment.shape
    taps = weight.shape[0]
    width = inner_proj.shape[2]
    wire = upstream.astype(jnp.bfloat16)
    out_grad = jnp.einsum("scq,scd->qd", normal, wire, preferred_element_type=jnp.float32)
    back_normal = jnp.einsum("scd,qd->scq", wire, out_proj, preferred_element_type=jnp.float32)
    _, pull_norm = jax.vjp(gate_norm, gated, total, gate_gain)
    back_gated, back_total, gate_grad = pull_norm(back_normal)
    back_total = lax.psum(back_total, "head")
    back_gated = back_gated + 2.0 * gated * back_total[..., None]
    _, pull_gate = jax.vjp(gated_out, output, entry, cstate, carried, gate)
    back_output, back_entry, back_cread, back_carried, back_gate = pull_gate(back_gated)
    later = entering(
        (carry, back_carried),
        "ctx",
        chain,
        (jnp.ones_like(carry), jnp.zeros_like(back_carried)),
        True,
    )[1]
    back_carry = jnp.sum(later * carried, axis=(2, 3))
    _, pull_mix = jax.vjp(
        partial(local_mixer, segment=segment, before=before),
        inner,
        bstate,
        cstate,
        steps_wide,
        step_bias,
        decay_log,
        skip_gain,
    )
    back_inner, back_bstate, back_cstate, back_steps, step_bias_grad, decay_grad, skip_grad = (
        pull_mix((back_output, back_entry, later, back_carry))
    )
    summed = lax.psum(jnp.concatenate([back_bstate, back_cstate + back_cread], axis=2), "head")
    back_active = jnp.concatenate([back_inner.reshape(batch, count, width), summed], axis=2)
    _, pull_conv = jax.vjp(partial(conv_act, labels=labels, segment=segment), window, weight, bias)
    back_window, kernel_grad, bias_grad = pull_conv(back_active)
    incoming = from_behind(back_window[:, : taps - 1], "ctx", -1)
    back_stack = back_window[:, taps - 1 :] + jnp.pad(
        incoming, ((0, 0), (count - taps + 1, 0), (0, 0))
    )
    back_both = jnp.stack(
        [back_gate.astype(jnp.bfloat16), back_stack[..., :width].astype(jnp.bfloat16)], axis=2
    )
    back_state = back_stack[..., width:].astype(jnp.bfloat16)
    back_narrow = back_steps.astype(jnp.bfloat16)
    inner_grad = jnp.einsum("scd,sckq->dkq", normed, back_both, preferred_element_type=jnp.float32)
    state_grad = jnp.einsum("scd,scn->dn", normed, back_state, preferred_element_type=jnp.float32)
    step_grad = jnp.einsum("scd,sch->dh", normed, back_narrow, preferred_element_type=jnp.float32)
    share = state_proj.shape[1] // lax.axis_size("head")
    start = lax.axis_index("head") * share
    part = jnp.einsum("sckq,dkq->scd", back_both, inner_proj, preferred_element_type=jnp.float32)
    part = part + jnp.einsum(
        "sch,dh->scd", back_narrow, step_proj, preferred_element_type=jnp.float32
    )
    part = part + jnp.einsum(
        "scn,dn->scd",
        lax.dynamic_slice_in_dim(back_state, start, share, 2),
        lax.dynamic_slice_in_dim(state_proj, start, share, 1),
        preferred_element_type=jnp.float32,
    )
    back_normed = lax.psum(part, "head")
    _, pull_pre = jax.vjp(scaled_norm, residual, norm_gain)
    back_residual, norm_grad = pull_pre(back_normed)
    matrices = (inner_grad, state_grad, step_grad, out_grad)
    others = (norm_grad, kernel_grad, bias_grad, step_bias_grad, decay_grad, skip_grad, gate_grad)
    return (upstream + back_residual, matrices, others)


def on_device(
    tokens,
    segments,
    cotangent,
    inner_proj,
    state_proj,
    step_proj,
    out_proj,
    norm_gain,
    mix_kernel,
    mix_bias,
    state_kernel,
    state_bias,
    step_bias,
    decay_log,
    skip_gain,
    gate_gain,
):
    layers = inner_proj.shape[0]
    taps = mix_kernel.shape[1]
    count = segments.shape[1]
    width = inner_proj.shape[3]
    heads = step_proj.shape[2]
    previous = from_behind(segments[:, count - taps + 1 :], "ctx", 1)
    labels = jnp.concatenate([previous, segments], axis=1)
    residual = tokens.astype(jnp.float32)
    fulls = []
    smalls = []
    saved = []
    for layer in range(layers):
        full = (
            lax.all_gather(inner_proj[layer], ("dp", "ctx"), axis=0, tiled=True),
            lax.all_gather(state_proj[layer], ("dp", "ctx"), axis=0, tiled=True),
            lax.all_gather(step_proj[layer], ("dp", "ctx"), axis=0, tiled=True),
            lax.all_gather(out_proj[layer], ("dp", "ctx"), axis=1, tiled=True),
        )
        small = (
            norm_gain[layer],
            mix_kernel[layer],
            mix_bias[layer],
            state_kernel[layer],
            state_bias[layer],
            step_bias[layer],
            decay_log[layer],
            skip_gain[layer],
            gate_gain[layer],
        )
        residual, kept = layer_forward(residual, segments, labels, full, small)
        fulls.append(full)
        smalls.append(small)
        saved.append(kept)
    mixed = residual.astype(jnp.bfloat16)
    upstream = cotangent.astype(jnp.float32)
    shards = [None] * layers
    others = [None] * layers
    for layer in reversed(range(layers)):
        upstream, matrices, others[layer] = layer_backward(
            upstream, segments, labels, fulls[layer], smalls[layer], saved[layer]
        )
        shards[layer] = matrices
    stacked_inner = jnp.stack([shards[index][0] for index in range(layers)])
    stacked_state = jnp.stack([shards[index][1] for index in range(layers)])
    stacked_step = jnp.stack([shards[index][2] for index in range(layers)])
    stacked_out = jnp.stack([shards[index][3] for index in range(layers)])
    reduced = (
        lax.psum_scatter(stacked_inner, ("dp", "ctx"), scatter_dimension=1, tiled=True),
        lax.psum_scatter(stacked_state, ("dp", "ctx"), scatter_dimension=1, tiled=True),
        lax.psum_scatter(stacked_step, ("dp", "ctx"), scatter_dimension=1, tiled=True),
        lax.psum_scatter(stacked_out, ("dp", "ctx"), scatter_dimension=2, tiled=True),
    )
    parts = lax.axis_size("head")
    where = lax.axis_index("head")

    def spread(piece):
        size = piece.shape[-1]
        wide = jnp.zeros(piece.shape[:-1] + (size * parts,), jnp.float32)
        return lax.dynamic_update_slice_in_dim(wide, piece, where * size, piece.ndim - 1)

    def narrow(whole, size):
        return lax.dynamic_slice_in_dim(whole, where * size, size, whole.ndim - 1)

    halve = 1.0 / parts
    norm_all = halve * jnp.stack([others[index][0] for index in range(layers)])
    kernel_all = jnp.stack([others[index][1] for index in range(layers)])
    bias_all = jnp.stack([others[index][2] for index in range(layers)])
    step_all = spread(jnp.stack([others[index][3] for index in range(layers)]))
    decay_all = spread(jnp.stack([others[index][4] for index in range(layers)]))
    skip_all = spread(jnp.stack([others[index][5] for index in range(layers)]))
    gate_all = spread(jnp.stack([others[index][6] for index in range(layers)]))
    totals = lax.psum(
        (
            norm_all,
            spread(kernel_all[..., :width]),
            spread(bias_all[..., :width]),
            halve * kernel_all[..., width:],
            halve * bias_all[..., width:],
            step_all,
            decay_all,
            skip_all,
            gate_all,
        ),
        ("dp", "ctx", "head"),
    )
    return (
        mixed,
        upstream.astype(jnp.bfloat16),
        reduced[0],
        reduced[1],
        reduced[2],
        reduced[3],
        totals[0],
        narrow(totals[1], width),
        narrow(totals[2], width),
        totals[3],
        totals[4],
        narrow(totals[5], heads),
        narrow(totals[6], heads),
        narrow(totals[7], heads),
        narrow(totals[8], width),
    )


def solution(mesh):
    return jax.shard_map(
        on_device,
        mesh=mesh,
        in_specs=(
            P("dp", "ctx", None),
            P("dp", "ctx"),
            P("dp", "ctx", None),
            P(None, ("dp", "ctx"), None, "head"),
            P(None, ("dp", "ctx"), None),
            P(None, ("dp", "ctx"), "head"),
            P(None, "head", ("dp", "ctx")),
            P(),
            P(None, None, "head"),
            P(None, "head"),
            P(),
            P(),
            P(None, "head"),
            P(None, "head"),
            P(None, "head"),
            P(None, "head"),
        ),
        out_specs=(
            P("dp", "ctx", None),
            P("dp", "ctx", None),
            P(None, ("dp", "ctx"), None, "head"),
            P(None, ("dp", "ctx"), None),
            P(None, ("dp", "ctx"), "head"),
            P(None, "head", ("dp", "ctx")),
            P(),
            P(None, None, "head"),
            P(None, "head"),
            P(),
            P(),
            P(None, "head"),
            P(None, "head"),
            P(None, "head"),
            P(None, "head"),
        ),
        check_vma=False,
    )
```

profile of v0, /device:TPU:0, one launch (start us, length us, event | category | flops | bytes accessed | tf_op | source)
XLA Modules:
  0.0 2048.2 jit_solution(14577304092568256592)
XLA Ops:
  16.1 47.8 %all-gather.2 = bf16[1,1024,16]{2,0,1:T(2,128)(2,1)S(1)} all-gather(bf16[1,64,16]{2,0,1:T(2,128)(2,1)S(1)} %copy.293), channel_id=4, replica_groups=mesh['dp'=4,'ctx'=4,'head'=2] {'dp','ctx'}, dimensions={1}, use_global_device_ids=true | all-gather | bytes 34816 | tf_op jit(solution)/shard_map/all_gather | solution.py:306
  66.0 45.9 %all-gather.1 = bf16[1,1024,256]{2,1,0:T(8,128)(2,1)S(1)} all-gather(bf16[1,64,256]{2,1,0:T(8,128)(2,1)S(1)} %get-tuple-element.2271), channel_id=3, replica_groups=mesh['dp'=4,'ctx'=4,'head'=2] {'dp','ctx'}, dimensions={1}, use_global_device_ids=true | all-gather | bytes 557056 | tf_op jit(solution)/shard_map/all_gather | solution.py:305
  134.2 30.8 %while.146 = (s32[]{:T(128)}, f32[2,256,16,64]{1,3,2,0:T(8,128)}, f32[2,256,16]{1,2,0:T(8,128)S(1)}, f32[2,16,64,128]{3,2,1,0:T(8,128)}, f32[2,16]{1,0:T(2,128)S...) while((s32[]{:T(128)}, f32[2,256,16,64]{1,3,2,0:T(8,128)}, ...), condition=%wide.region_4.5_spmd, body=%wide.region_1.4_spmd.sunk | while | flops 1314972672 | bytes 6601659 | solution.py:84
  172.5 11.6 all-gather.14
  184.1 60.4 %all-gather.27.cloned.1.call-done = f32[8,16,64,128]{3,2,1,0:T(8,128)} async-done(((f32[2,16,64,128]{3,2,1,0:T(8,128)}), f32[8,16,64,128]{3,2,1,0:T(8,128)}) %all-gather.27.cloned.1.call-update) | async-done | bytes 4194320 | tf_op jit(solution)/shard_map/all_gather | solution.py:23
  261.8 45.3 %all-gather.29.cloned.1.call-done = bf16[1,1024,1024]{1,2,0:T(8,128)(2,1)} async-done(((bf16[1,1024,64]{1,2,0:T(8,128)(2,1)}), bf16[1,1024,1024]{1,2,0:T(8,128)(2,1)}) %all-gather.29.cloned.1.call-update) | async-done | bytes 2097168 | tf_op jit(solution)/shard_map/all_gather | solution.py:307
  312.4 44.5 %all-gather.8 = bf16[1,1024,16]{2,0,1:T(2,128)(2,1)S(1)} all-gather(bf16[1,64,16]{2,0,1:T(2,128)(2,1)S(1)} %copy.295), channel_id=10, replica_groups=mesh['dp'=4,'ctx'=4,'head'=2] {'dp','ctx'}, dimensions={1}, use_global_device_ids=true | all-gather | bytes 34816 | tf_op jit(solution)/shard_map/all_gather | solution.py:306
  357.3 45.7 %all-gather.7 = bf16[1,1024,256]{2,1,0:T(8,128)(2,1)S(1)} all-gather(bf16[1,64,256]{2,1,0:T(8,128)(2,1)S(1)} %get-tuple-element.2270), channel_id=9, replica_groups=mesh['dp'=4,'ctx'=4,'head'=2] {'dp','ctx'}, dimensions={1}, use_global_device_ids=true | all-gather | bytes 557056 | tf_op jit(solution)/shard_map/all_gather | solution.py:305
  438.9 37.9 %while.147 = (s32[]{:T(128)}, f32[2,256,16,64]{1,3,2,0:T(8,128)}, f32[2,256,16]{1,2,0:T(8,128)S(1)}, f32[2,16,64,128]{3,2,1,0:T(8,128)}, f32[2,16]{1,0:T(2,128)S...) while((s32[]{:T(128)}, f32[2,256,16,64]{1,3,2,0:T(8,128)}, ...), condition=%wide.region_14.15_spmd, body=%wide.region_11.14_spmd.sunk | while | flops 1314972672 | bytes 6601659 | solution.py:84
  493.7 63.8 %all-gather.33.cloned.1.call-done = f32[8,16,64,128]{3,2,1,0:T(8,128)} async-done(((f32[2,16,64,128]{3,2,1,0:T(8,128)}), f32[8,16,64,128]{3,2,1,0:T(8,128)}) %all-gather.33.cloned.1.call-update) | async-done | bytes 4194320 | tf_op jit(solution)/shard_map/all_gather | solution.py:23
  577.8 42.7 %all-gather.35.cloned.1.call-done = bf16[1,1024,1024]{1,2,0:T(8,128)(2,1)} async-done(((bf16[1,1024,64]{1,2,0:T(8,128)(2,1)}), bf16[1,1024,1024]{1,2,0:T(8,128)(2,1)}) %all-gather.35.cloned.1.call-update) | async-done | bytes 2097168 | tf_op jit(solution)/shard_map/all_gather | solution.py:307
  651.9 69.9 %all-gather.37.cloned.1.call-done = f32[8,16,64,128]{3,2,1,0:T(8,128)} async-done(((f32[2,16,64,128]{3,2,1,0:T(8,128)}), f32[8,16,64,128]{3,2,1,0:T(8,128)}) %all-gather.37.cloned.1.call-update) | async-done | bytes 4194320 | tf_op jit(solution)/shard_map/all_gather | solution.py:23
  739.6 83.5 %while.151 = (s32[]{:T(128)}, f32[16]{0:T(128)}, f32[16]{0:T(128)}, f32[16]{0:T(128)}, f32[2,256,16,64]{1,3,2,0:T(8,128)}, /*index=5*/f32[2,256,128]{2,1,0:T(8,1...) while((s32[]{:T(128)}, f32[16]{0:T(128)}, f32[16]{0:T(128)}, ...), condition=%wide.region_39.41_spmd.clone, body=%wide.region_26.40_spmd.clone.sunk | while | flops 2739069952 | bytes 45194912 | solution.py:84
  830.8 12.6 all-reduce.35.cloned.1.call-done
  863.2 21.5 %all-reduce.37.cloned.1.call-done = f32[2,256,1024]{2,1,0:T(8,128)} async-done(((f32[2,256,1024]{2,1,0:T(8,128)}), f32[2,256,1024]{2,1,0:T(8,128)}) %all-reduce.37.cloned.1.call-update) | async-done | bytes 2097168 | tf_op jit(solution)/shard_map/psum | solution.py:265
  922.2 67.1 %all-gather.39.cloned.1.call-done = f32[8,16,64,128]{3,2,1,0:T(8,128)} async-done(((f32[2,16,64,128]{3,2,1,0:T(8,128)}), f32[8,16,64,128]{3,2,1,0:T(8,128)}) %all-gather.39.cloned.1.call-update) | async-done | bytes 4194320 | tf_op jit(solution)/shard_map/all_gather | solution.py:23
  1006.9 77.8 %while.153 = (s32[]{:T(128)}, f32[16]{0:T(128)}, f32[16]{0:T(128)}, f32[16]{0:T(128)}, f32[2,256,16,64]{1,3,2,0:T(8,128)}, /*index=5*/f32[2,256,128]{2,1,0:T(8,1...) while((s32[]{:T(128)}, f32[16]{0:T(128)}, f32[16]{0:T(128)}, ...), condition=%wide.region_62.64_spmd.clone, body=%wide.region_49.63_spmd.clone.sunk | while | flops 2739069952 | bytes 26189164 | solution.py:84
  1120.1 13.4 copy.253
  1187.3 119.3 %all-reduce.41.cloned.1.call-done = f32[2,4,2048]{2,1,0:T(4,128)} async-done(((f32[2,4,2048]{2,1,0:T(4,128)}), f32[2,4,2048]{2,1,0:T(4,128)}) %all-reduce.41.cloned.1.call-update) | async-done | bytes 65552 | tf_op jit(solution)/shard_map/psum | solution.py:362
  1308.0 262.6 %all-reduce.43.cloned.1.call-done = f32[2,1024,1024]{1,0,2:T(2,128)} async-done(((f32[2,1024,1024]{1,0,2:T(2,128)}), f32[2,1024,1024]{1,0,2:T(2,128)}) %all-reduce.43.cloned.1.call-update) | async-done | bytes 8388624
  1572.7 28.0 %all-reduce.45.cloned.1.call-done = (f32[2,256,1024]{2,1,0:T(8,128)}, f32[2,256,1024]{2,1,0:T(8,128)}) async-done(((f32[2,256,1024]{2,1,0:T(8,128)}, f32[2,256,1024]{2,1,0:T(8,128)}), (f32[2,256,1024]{2,1,0:T(8,128)}, f32[2,256,1024]{2,1,0:T(8,128)})) %all-reduce.45.cloned.1.call-update) | async-done | bytes 4194320 | tf_op jit(solution)/shard_map/psum | solution.py:147
  1603.0 49.1 %all-reduce.23 = (f32[2,1024]{1,0:T(2,128)}, f32[2,2048]{1,0:T(2,128)S(1)}, f32[2,4,256]{2,1,0:T(4,128)}, f32[2,256]{1,0:T(2,128)}, f32[2,32]{1,0:T(2,128)S(1)},...) all-reduce(f32[2,1024]{1,0:T(2,128)S(1)} %maximum_multiply_fusion, ...), channel_id=1, replica_groups=mesh['dp'=4,'ctx'=4,'head'=2] {'dp','ctx','head'}, use_global_device_ids=true, to_apply=%region_72.74 | all-reduce | flops 12992 | bytes 103936 | tf_op jit(solution)/shard_map/psum | solution.py:362
  1659.9 295.1 %reduce-scatter.6.cloned.1.call-done = f32[2,64,2,1024]{3,1,2,0:T(8,128)} async-done(((f32[2,1024,2,1024]{3,1,2,0:T(8,128)}), f32[2,64,2,1024]{3,1,2,0:T(8,128)}) %reduce-scatter.6.cloned.1.call-update) | async-done | bytes 1048592 | tf_op jit(solution)/shard_map/reduce_scatter | solution.py:338
  1958.1 83.1 %reduce-scatter.8.cloned.1.call-done = f32[2,64,256]{2,1,0:T(8,128)} async-done(((f32[2,1024,256]{2,1,0:T(8,128)}), f32[2,64,256]{2,1,0:T(8,128)}) %reduce-scatter.8.cloned.1.call-update) | async-done | bytes 131088 | tf_op jit(solution)/shard_map/reduce_scatter | solution.py:339
  (1018 shorter events, 616.2 us)
Async XLA Ops:
  7.3 106.5 %all-gather.25.cloned.1.call-start = ((), (), s32[]{:S(2)}) async-start(), calls=%async_computation.10 | async-start | bytes 4456448 | tf_op jit(solution)/shard_map/all_gather | solution.py:304
  9.6 234.9 %all-gather.27.cloned.1.call-start = ((), (), s32[]{:S(2)}) async-start(), calls=%async_computation.11 | async-start | bytes 5242880 | tf_op jit(solution)/shard_map/all_gather | solution.py:23
  10.4 102.5 %collective-permute-start.1 = (s32[2,3]{1,0:T(2,128)S(1)}, s32[2,3]{1,0:T(2,128)S(1)}, u32[]{:S(2)}, u32[]{:S(2)}) collective-permute-start(s32[2,3]{1,0:T(2,128)S(1)} %slice.414), channel_id=1, source_target_pairs={{0,2},{2,4},{4,6},{1,3},{3,5},{5,7},{8,10},{10,12},{12,14},{9,11},... | collective-permute-start | bytes 80 | tf_op jit(solution)/shard_map/ppermute | solution.py:18
  118.6 4.7 collective-permute-start
  165.1 142.0 %all-gather.29.cloned.1.call-start = ((), (), s32[]{:S(2)}) async-start(), calls=%async_computation.12 | async-start | bytes 2228224 | tf_op jit(solution)/shard_map/all_gather | solution.py:307
  166.1 236.9 %all-reduce.33.cloned.1.call-start = ((), (), s32[]{:S(2)}) async-start(), calls=%async_computation.3 | async-start | bytes 4194304 | tf_op jit(solution)/shard_map/psum | solution.py:147
  166.2 464.1 %copy-start.89 = (f32[1,1024]{1,0:T(1,128)}, f32[1,1024]{1,0:T(1,128)S(1)}, u32[]{:S(2)}) copy-start(f32[1,1024]{1,0:T(1,128)S(1)} %get-tuple-element.2276) | copy-start | bytes 12292
  311.4 104.8 %all-gather.31.cloned.1.call-start = ((), (), s32[]{:S(2)}) async-start(), calls=%async_computation.13 | async-start | bytes 4456448 | tf_op jit(solution)/shard_map/all_gather | solution.py:304
  312.3 245.2 %all-gather.33.cloned.1.call-start = ((), (), s32[]{:S(2)}) async-start(), calls=%async_computation.14 | async-start | bytes 5242880 | tf_op jit(solution)/shard_map/all_gather | solution.py:23
  422.7 5.3 collective-permute-start.2
  476.8 143.7 %all-gather.35.cloned.1.call-start = ((), (), s32[]{:S(2)}) async-start(), calls=%async_computation.15 | async-start | bytes 2228224 | tf_op jit(solution)/shard_map/all_gather | solution.py:307
  477.5 244.3 %all-gather.37.cloned.1.call-start = ((), (), s32[]{:S(2)}) async-start(), calls=%async_computation.16 | async-start | bytes 5242880 | tf_op jit(solution)/shard_map/all_gather | solution.py:23
  642.2 201.2 %all-reduce.35.cloned.1.call-start = ((), (), s32[]{:S(2)}) async-start(), calls=%async_computation.4 | async-start | bytes 1048576 | tf_op jit(solution)/shard_map/psum | solution.py:237
  826.0 58.7 %all-reduce.37.cloned.1.call-start = ((), (), s32[]{:S(2)}) async-start(), calls=%async_computation.5 | async-start | bytes 4194304 | tf_op jit(solution)/shard_map/psum | solution.py:265
  849.6 5.9 collective-permute-start.3
  863.2 126.1 %all-gather.39.cloned.1.call-start = ((), (), s32[]{:S(2)}) async-start(), calls=%async_computation.17 | async-start | bytes 5242880 | tf_op jit(solution)/shard_map/all_gather | solution.py:23
  907.2 198.1 %all-reduce.39.cloned.1.call-start = ((), (), s32[]{:S(2)}) async-start(), calls=%async_computation.6 | async-start | bytes 1048576 | tf_op jit(solution)/shard_map/psum | solution.py:237
  1087.8 97.9 %reduce-scatter.10.cloned.1.call-start = ((), (), s32[]{:S(2)}) async-start(), calls=%async_computation.18 | async-start | bytes 557056
  1100.2 206.4 %all-reduce.41.cloned.1.call-start = ((), (), s32[]{:S(2)}) async-start(), calls=%async_computation.9 | async-start | bytes 131072 | tf_op jit(solution)/shard_map/psum | solution.py:362
  1111.6 459.0 %all-reduce.43.cloned.1.call-start = ((), (), s32[]{:S(2)}) async-start(), calls=%async_computation.19 | async-start | bytes 16777216
  1133.6 467.1 %all-reduce.45.cloned.1.call-start = ((), (), s32[]{:S(2)}) async-start(), calls=%async_computation.20 | async-start | bytes 8388608 | tf_op jit(solution)/shard_map/psum | solution.py:147
  1141.1 6.2 collective-permute-start.4
  1155.1 800.0 %reduce-scatter.6.cloned.1.call-start = ((), (), s32[]{:S(2)}) async-start(), calls=%async_computation.7 | async-start | bytes 17825792 | tf_op jit(solution)/shard_map/reduce_scatter | solution.py:338
  1169.0 872.1 %reduce-scatter.8.cloned.1.call-start = ((), (), s32[]{:S(2)}) async-start(), calls=%async_computation.8 | async-start | bytes 2228224 | tf_op jit(solution)/shard_map/reduce_scatter | solution.py:339
  (239 other events, 4291.0 us)
Sparse Core Ops, SparseCore 0:
  11.5 85.9 all-gather.24
  165.2 79.2 all-gather.26
  247.9 59.2 all-gather.28
  311.6 19.8 all-reduce.32
  335.1 81.1 all-gather.30
  476.9 80.5 all-gather.32
  561.2 59.1 all-gather.34
  642.3 79.3 all-gather.36
  826.2 17.2 all-reduce.34
  863.3 21.4 all-reduce.36
  907.3 81.9 all-gather.38
  1087.9 17.2 all-reduce.38
  1107.5 78.1 reduce-scatter.9
  1192.6 113.9 all-reduce.40
  1313.5 257.0 all-reduce.42
  1573.1 27.4 all-reduce.44
  1602.8 352.2 reduce-scatter.5
  1957.8 83.3 reduce-scatter.7
where the time goes:
time: 2060 us; the launch traced here: 2050 us
  waiting for transfers between devices  1210 us (59%)
  blocking collectives  265 us (13%)
  matrix products  193 us (9%)
  other arithmetic  170 us (8%)
  local copies, waits for them, and re-layouts  168 us (8%)
    reduce_scatter x1, waiting for transfers between devices, on_device(): lax.psum_scatter(stacked_inner, ('dp', 'ctx'), scatter_dimension=1, tiled...  295 us
    unnamed x20, waiting for transfers between devices  273 us
    all_gather x4, waiting for transfers between devices, entering(): pieces = jax.tree.map(lambda part: lax.all_gather(part, axis), value)  261 us
    psum x1, waiting for transfers between devices, on_device(): lax.psum((norm_all, spread(kernel_all[..., :width]), spread(bias_all[...,...  119 us
    all_gather x2, blocking collectives, on_device(): lax.all_gather(step_proj[layer], ('dp', 'ctx'), axis=0, tiled=True)  92.3 us
    all_gather x2, blocking collectives, on_device(): lax.all_gather(state_proj[layer], ('dp', 'ctx'), axis=0, tiled=True)  91.6 us
    all_gather x2, waiting for transfers between devices, on_device(): lax.all_gather(out_proj[layer], ('dp', 'ctx'), axis=1, tiled=True)  88 us
    reduce_scatter x1, waiting for transfers between devices, on_device(): lax.psum_scatter(stacked_state, ('dp', 'ctx'), scatter_dimension=1, tiled...  83.1 us
  transfers between devices with their start and end apart: 23, of which 19 were waited for; matrix products, arithmetic and copies ran while one was open for 8% of the time, Pallas kernels for 0%

commit v1 on v0

v1 whole, which is shorter than its diff:
```python
import jax
import jax.numpy as jnp
from jax import lax
from jax.experimental import pallas as pl
from jax.experimental.pallas import tpu as pltpu
from jax.sharding import PartitionSpec as P

EPSILON = 1e-05
F32 = jnp.float32
BF16 = jnp.bfloat16
HIGH = lax.Precision.HIGHEST
CHUNK = 128
LANES = 128
RIM = 8
FAR = -1e30


def mm(a, b, ca=1, cb=0, precision=None):
    return lax.dot_general(
        a, b, (((ca,), (cb,)), ((), ())), precision=precision, preferred_element_type=F32
    )


def split_mm(a, b, ca=1, cb=0):
    top = a.astype(BF16)
    rest = (a - top.astype(F32)).astype(BF16)
    return mm(top, b, ca, cb) + mm(rest, b, ca, cb)


def mm_split(a, b, ca=1, cb=0):
    top = b.astype(BF16)
    rest = (b - top.astype(F32)).astype(BF16)
    return mm(a, top, ca, cb) + mm(a, rest, ca, cb)


def kernel_call(body, outs, scratch, *args):
    return pl.pallas_call(
        body,
        out_shape=outs,
        scratch_shapes=scratch,
        compiler_params=pltpu.CompilerParams(vmem_limit_bytes=48 * 1024 * 1024),
    )(*args)


def grid_masks():
    row = lax.broadcasted_iota(jnp.int32, (CHUNK, CHUNK), 0)
    col = lax.broadcasted_iota(jnp.int32, (CHUNK, CHUNK), 1)
    return row, col


def soft(v):
    return jnp.maximum(v, 0.0) + jnp.log1p(jnp.exp(-jnp.abs(v)))


def sigmoid(v):
    return 1.0 / (1.0 + jnp.exp(-v))


def conv_body(
    raw_ref, halo_ref, traw_ref, info_ref, taps_ref, perhead_ref, spread_ref,
    act_ref, delta_ref, acc_ref, state_ref, total_ref, window,
):
    count, wide = raw_ref.shape
    chunks = count // CHUNK
    width = spread_ref.shape[1]
    row, col = grid_masks()
    tri = (row >= col).astype(F32)
    totals = []
    for c in range(chunks):
        rows = pl.ds(c * CHUNK, CHUNK)
        delta = soft(traw_ref[rows, :] + perhead_ref[0:1, :])
        rate = -delta * jnp.exp(perhead_ref[1:2, :])
        acc = mm(tri, rate, precision=HIGH)
        delta_ref[rows, :] = delta
        acc_ref[rows, :] = acc
        totals.append(acc[CHUNK - 1 : CHUNK, :])
    whole = totals[0]
    for c in range(1, chunks):
        whole = whole + totals[c]
    total_ref[...] = jnp.broadcast_to(
        jnp.exp(whole) * info_ref[count - 1 : count, 6:7], total_ref.shape
    )

    def block(cb, _):
        lanes = pl.ds(pl.multiple_of(cb * LANES, LANES), LANES)
        window[0:RIM, :] = halo_ref[:, lanes].astype(F32)
        window[RIM : RIM + count, :] = raw_ref[:, lanes].astype(F32)
        taps = taps_ref[:, lanes]
        for c in range(chunks):
            base = c * CHUNK
            pre = taps[4:5, :] + taps[3:4, :] * window[RIM + base : RIM + base + CHUNK, :]
            for d in (1, 2, 3):
                moved = window[RIM + base - d : RIM + base - d + CHUNK, :]
                pre = pre + taps[3 - d : 4 - d, :] * (
                    moved * info_ref[base : base + CHUNK, d : d + 1]
                )
            act_ref[base : base + CHUNK, lanes] = (pre * sigmoid(pre)).astype(BF16)
        return 0

    lax.fori_loop(0, wide // LANES, block, 0)
    spread = spread_ref[...]
    state = jnp.zeros((LANES, width), F32)
    after = jnp.zeros_like(totals[0])
    for c in reversed(range(chunks)):
        rows = pl.ds(c * CHUNK, CHUNK)
        weight = (
            jnp.exp(totals[c] - acc_ref[rows, :] + after) * info_ref[rows, 7:8] * delta_ref[rows, :]
        )
        scaled = act_ref[rows, 0:width].astype(F32) * split_mm(weight, spread)
        state = state + mm_split(act_ref[rows, width : width + LANES], scaled, 0, 0)
        after = after + totals[c]
    state_ref[...] = state


def chunk_terms(c, acc_ref, info_ref, segrow_ref):
    rows = pl.ds(pl.multiple_of(c * CHUNK, CHUNK), CHUNK)
    acc = acc_ref[rows, :]
    row, col = grid_masks()
    same = (info_ref[rows, 0:1] == segrow_ref[0:1, rows]) & (row >= col)
    blocked = jnp.where(same, 0.0, FAR)
    total = acc[CHUNK - 1 : CHUNK, :]
    flags = info_ref[rows, :]
    entry = jnp.exp(acc) * flags[:, 4:5]
    tail = jnp.exp(total - acc) * flags[:, 5:6]
    carry = jnp.exp(total) * flags[CHUNK - 1 : CHUNK, 4:5]
    return rows, acc, acc.T, blocked, entry, tail, carry


def mix_body(
    act_ref, delta_ref, acc_ref, info_ref, segrow_ref, perhead_ref, spread_ref, start_ref,
    gate_ref, gain_ref, y_ref, scaled_ref, squares_ref, states_ref, state,
):
    count, width = gate_ref.shape
    spread = spread_ref[...]
    state[...] = start_ref[...].astype(F32)
    skip = split_mm(perhead_ref[...], spread)[2:3, :]
    lane = lax.broadcasted_iota(jnp.int32, (CHUNK, LANES), 1)
    low_half = lane < LANES // 2

    def step(c, _):
        rows, acc, across, blocked, entry, tail, carry = chunk_terms(
            c, acc_ref, info_ref, segrow_ref
        )
        now = state[...]
        now_low = now.astype(BF16)
        states_ref[pl.ds(pl.multiple_of(c * LANES, LANES), LANES), :] = now_low
        bstate = act_ref[rows, width : width + LANES]
        cstate = act_ref[rows, width + LANES : width + 2 * LANES]
        gram = mm(cstate, bstate, 1, 1)
        x = act_ref[rows, 0:width].astype(F32)
        scaled = x * split_mm(delta_ref[rows, :], spread)
        z = scaled.astype(BF16)
        y_ref[rows, :] = split_mm(entry, spread) * mm_split(cstate, now) + skip * x
        tailed = scaled * split_mm(tail, spread)
        state[...] = split_mm(carry, spread) * now + mm_split(bstate, tailed, 0, 0)
        squares = jnp.zeros((CHUNK, LANES), F32)
        for pair in range(width // LANES):
            lanes = slice(pair * LANES, (pair + 1) * LANES)
            zb = z[:, lanes]
            out = y_ref[rows, lanes]
            for half in (0, 1):
                h = 2 * pair + half
                decay = jnp.exp(acc[:, h : h + 1] - across[h : h + 1, :] + blocked)
                keep = low_half if half == 0 else jnp.logical_not(low_half)
                zh = jnp.where(keep, zb, jnp.zeros_like(zb))
                zl = (jnp.where(keep, scaled[:, lanes], 0.0) - zh.astype(F32)).astype(BF16)
                mat = gram * decay
                top = mat.astype(BF16)
                rest = (mat - top.astype(F32)).astype(BF16)
                out = out + mm(top, zh) + mm(rest, zh) + mm(top, zl)
            y_ref[rows, lanes] = out
            gate = gate_ref[rows, lanes]
            gated = out * (gate * sigmoid(gate))
            squares = squares + gated * gated
            scaled_ref[rows, lanes] = gated
        squares_ref[rows, :] = jnp.broadcast_to(
            jnp.sum(squares, axis=1, keepdims=True), (CHUNK, LANES)
        )
        return 0

    lax.fori_loop(0, count // CHUNK, step, 0)


def gate_body(
    bn_ref, y_ref, gate_ref, gain_ref, factor_ref, act_ref, acc_ref, info_ref, spread_ref,
    dy_ref, dgate_ref, ggrad_ref, state_ref,
):
    count, width = bn_ref.shape
    chunks = count // CHUNK
    spread = spread_ref[...]
    state = jnp.zeros((LANES, width), F32)
    before = jnp.zeros((1, LANES), F32)
    sums = jnp.zeros((1, width), F32)
    for c in range(chunks):
        rows = slice(c * CHUNK, (c + 1) * CHUNK)
        bn = bn_ref[rows, :]
        y = y_ref[rows, :]
        gate = gate_ref[rows, :]
        root = factor_ref[rows, 0:1]
        coef = factor_ref[rows, 1:2]
        sig = sigmoid(gate)
        silu = gate * sig
        gated = y * silu
        back = root * (bn * gain_ref[0:1, :]) - gated * coef
        dy = back * silu
        dy_ref[rows, :] = dy.astype(BF16)
        dgate_ref[rows, :] = (back * y * (sig * (1.0 + gate * (1.0 - sig)))).astype(BF16)
        sums = sums + jnp.sum(bn * gated * root, axis=0, keepdims=True)
        acc = acc_ref[rows, :]
        entry = jnp.exp(acc + before) * info_ref[rows, 6:7]
        cstate = act_ref[rows, width + LANES : width + 2 * LANES]
        state = state + mm(cstate, (dy * split_mm(entry, spread)).astype(BF16), 0, 0)
        before = before + acc[CHUNK - 1 : CHUNK, :]
    ggrad_ref[...] = jnp.broadcast_to(sums, ggrad_ref.shape)
    state_ref[...] = state.astype(BF16)


def back_body(
    act_ref, delta_ref, acc_ref, traw_ref, info_ref, segrow_ref, ahead_ref, perhead_ref, spread_ref,
    states_ref, later_ref, dy_ref, raw_ref, halo_ref, taps_ref,
    dv_ref, dvs_ref, rim_ref, last_ref, dtraw_ref, tapgrad_ref, headgrad_ref,
    dstate, dact, window, gradient,
):
    count, wide = raw_ref.shape
    width = spread_ref.shape[1]
    chunks = count // CHUNK
    spread = spread_ref[...]
    dstate[...] = later_ref[...].astype(F32)
    skip = split_mm(perhead_ref[...], spread)[2:3, :]
    row, col = grid_masks()
    upper = (row <= col).astype(F32)
    lower = (row > col).astype(F32)
    upper_low = upper.astype(BF16)
    lane = lax.broadcasted_iota(jnp.int32, (CHUNK, LANES), 1)
    low_half = lane < LANES // 2
    headgrad_ref[...] = jnp.zeros_like(headgrad_ref)
    decay_rate = jnp.exp(perhead_ref[1:2, :])

    def step(index, _):
        c = chunks - 1 - index
        rows, acc, across, blocked, entry, tail, carry = chunk_terms(
            c, acc_ref, info_ref, segrow_ref
        )
        delta = delta_ref[rows, :]
        bstate = act_ref[rows, width : width + LANES]
        cstate = act_ref[rows, width + LANES : width + 2 * LANES]
        gram = mm(cstate, bstate, 1, 1)
        x = act_ref[rows, 0:width].astype(F32)
        dy_low = dy_ref[rows, :]
        dy = dy_low.astype(F32)
        wide_delta = split_mm(delta, spread)
        scaled = x * wide_delta
        z = scaled.astype(BF16)
        later = dstate[...]
        later_low = later.astype(BF16)
        now_low = states_ref[pl.ds(pl.multiple_of(c * LANES, LANES), LANES), :]
        wide_tail = split_mm(tail, spread)
        tail_in = wide_tail * mm(bstate, later_low)
        entered = dy * split_mm(entry, spread)
        entered_low = entered.astype(BF16)
        from_entry = split_mm(entered * mm(cstate, now_low), spread, 1, 1)
        from_tail = split_mm(scaled * tail_in, spread, 1, 1)
        wide_carry = split_mm(carry, spread)
        kept = jnp.sum(later * now_low.astype(F32), axis=0, keepdims=True) * wide_carry
        from_carry = split_mm(jnp.broadcast_to(kept, (8, width)), spread, 1, 1)[0:1, :]
        dstate[...] = wide_carry * later + mm(cstate, entered_low, 0, 0)
        drate = (
            mm(upper, from_entry, precision=HIGH) + mm(lower, from_tail, precision=HIGH) + from_carry
        )
        dgram = jnp.zeros((CHUNK, CHUNK), F32)
        direct = jnp.zeros((CHUNK, LANES), F32)
        for pair in range(width // LANES):
            lanes = slice(pair * LANES, (pair + 1) * LANES)
            zb = z[:, lanes]
            dyb = dy_low[:, lanes]
            back = tail_in[:, lanes]
            for half in (0, 1):
                h = 2 * pair + half
                keep = low_half if half == 0 else jnp.logical_not(low_half)
                dyh = jnp.where(keep, dyb, jnp.zeros_like(dyb))
                decay = jnp.exp(acc[:, h : h + 1] - across[h : h + 1, :] + blocked)
                grad = mm(dyh, zb, 1, 1) * decay
                dgram = dgram + grad
                moved = mm(upper_low, (grad * gram).astype(BF16)) * lower
                drate = drate + jnp.where(lane == h, jnp.sum(moved, axis=1, keepdims=True), 0.0)
                back = back + mm((gram * decay).astype(BF16), dyh, 0, 0)
            direct = direct + split_mm(x[:, lanes] * back, spread[:, lanes], 1, 1)
            dact[rows, lanes] = wide_delta[:, lanes] * back + skip[:, lanes] * dy[:, lanes]
        dgram_low = dgram.astype(BF16)
        tailed = (scaled * wide_tail).astype(BF16)
        dact[rows, width : width + LANES] = mm(dgram_low, cstate, 0, 0) + mm(
            tailed, later_low, 1, 1
        )
        dact[rows, width + LANES : width + 2 * LANES] = mm(dgram_low, bstate) + mm(
            entered_low, now_low, 1, 1
        )
        ddelta = direct - decay_rate * drate
        dtraw = ddelta * sigmoid(traw_ref[rows, :] + perhead_ref[0:1, :])
        dtraw_ref[rows, :] = dtraw.astype(BF16)
        rate = -delta * decay_rate
        skipped = split_mm(x * dy, spread, 1, 1)
        headgrad_ref[0:1, :] += jnp.sum(dtraw, axis=0, keepdims=True)
        headgrad_ref[1:2, :] += jnp.sum(drate * rate, axis=0, keepdims=True)
        headgrad_ref[2:3, :] += jnp.sum(skipped, axis=0, keepdims=True)
        return 0

    lax.fori_loop(0, chunks, step, 0)
    gradient[0:RIM, :] = jnp.zeros((RIM, LANES), F32)
    gradient[RIM + count : 2 * RIM + count, :] = jnp.zeros((RIM, LANES), F32)

    def block(lanes, put):
        window[0:RIM, :] = halo_ref[:, lanes].astype(F32)
        window[RIM : RIM + count, :] = raw_ref[:, lanes].astype(F32)
        taps = taps_ref[:, lanes]
        sums = [jnp.zeros((1, LANES), F32) for _ in range(5)]
        for c in range(chunks):
            base = c * CHUNK
            moved = [window[RIM + base : RIM + base + CHUNK, :]]
            for d in (1, 2, 3):
                moved.append(
                    window[RIM + base - d : RIM + base - d + CHUNK, :]
                    * info_ref[base : base + CHUNK, d : d + 1]
                )
            pre = taps[4:5, :]
            for d in range(4):
                pre = pre + taps[3 - d : 4 - d, :] * moved[d]
            sig = sigmoid(pre)
            dpre = dact[base : base + CHUNK, lanes] * (sig * (1.0 + pre * (1.0 - sig)))
            gradient[RIM + base : RIM + base + CHUNK, :] = dpre
            for d in range(4):
                sums[3 - d] = sums[3 - d] + jnp.sum(dpre * moved[d], axis=0, keepdims=True)
            sums[4] = sums[4] + jnp.sum(dpre, axis=0, keepdims=True)
        for index in range(5):
            tapgrad_ref[index : index + 1, lanes] = sums[index]

        def pulled(base, size):
            out = taps[3:4, :] * gradient[base : base + size, :]
            for d in (1, 2, 3):
                out = out + taps[3 - d : 4 - d, :] * (
                    gradient[base + d : base + d + size, :] * ahead_ref[base : base + size, d : d + 1]
                )
            return out

        put(pulled, lanes)

    def put_x(pulled, lanes):
        rim_ref[:, lanes] = pulled(0, RIM)
        for c in range(chunks):
            back = pulled(RIM + c * CHUNK, CHUNK)
            dv_ref[c * CHUNK : (c + 1) * CHUNK, lanes] = back.astype(BF16)
            if c == chunks - 1:
                last_ref[:, lanes] = back[CHUNK - RIM :, :]

    def put_state(at):
        def put(pulled, lanes):
            dvs_ref[0:RIM, at : at + LANES] = pulled(0, RIM)
            for c in range(chunks):
                base = RIM + c * CHUNK
                dvs_ref[base : base + CHUNK, at : at + LANES] = pulled(base, CHUNK)

        return put

    def loop(cb, _):
        block(pl.ds(pl.multiple_of(cb * LANES, LANES), LANES), put_x)
        return 0

    lax.fori_loop(0, width // LANES, loop, 0)
    for at in range(0, wide - width, LANES):
        block(slice(width + at, width + at + LANES), put_state(at))
    tapgrad_ref[5:8, :] = jnp.zeros((3, wide), F32)


def swap(x, axis, bit):
    size = lax.axis_size(axis)
    return lax.ppermute(x, axis, [(i, i ^ bit) for i in range(size)])


def bits_of(axis):
    size = lax.axis_size(axis)
    return [1 << k for k in reversed(range(size.bit_length() - 1))]


def gather_near(x):
    for bit in bits_of("ctx"):
        x = jnp.concatenate([x, swap(x, "ctx", bit)], axis=0)
    return x


def gather_far(near):
    if lax.axis_size("dp") != 4:
        x = near
        for bit in reversed(bits_of("dp")):
            x = jnp.concatenate([x, swap(x, "dp", bit)], axis=0)
        return x
    half = near.shape[0] // 2
    one = swap(near, "dp", 1)
    two = swap(near, "dp", 2)
    three = [swap(one[:half], "dp", 2), swap(two[half:], "dp", 1)]
    return jnp.concatenate([near, one, two] + three, axis=0)


def scatter_rows(*matrices):
    count = lax.axis_size("dp")
    group = matrices[0].shape[0] // count

    def part(start, size):
        return jnp.concatenate([g[start : start + size] for g in matrices], axis=1)

    if count != 4:
        whole = part(0, count * group).astype(F32)
        for bit in bits_of("dp"):
            size = bit * group
            whole = whole[:size] + swap(whole[size:].astype(BF16), "dp", bit).astype(F32)
        near = whole
    else:
        half = group // 2
        far_one = swap(part(3 * group, half), "dp", 2).astype(F32)
        far_two = swap(part(3 * group + half, half), "dp", 1).astype(F32)
        none = jnp.zeros_like(far_one)
        one = part(group, group).astype(F32) + jnp.concatenate([far_one, none])
        two = part(2 * group, group).astype(F32) + jnp.concatenate([none, far_two])
        near = (
            part(0, group).astype(F32)
            + swap(one.astype(BF16), "dp", 1).astype(F32)
            + swap(two.astype(BF16), "dp", 2).astype(F32)
        )
    for bit in reversed(bits_of("ctx")):
        half = near.shape[0] // 2
        near = near[:half] + swap(near[half:].astype(BF16), "ctx", bit).astype(F32)
    return near


def total_over(x):
    for axis in ("ctx", "dp"):
        for bit in bits_of(axis):
            x = x + swap(x, axis, bit)
    return x


def head_sum(x):
    low = x.astype(BF16)
    return low.astype(F32) + swap(low, "head", 1).astype(F32)


def own_half(x, other=False):
    half = x.shape[-1] // 2
    first = (lax.axis_index("head") == 0) != other
    return jnp.where(first, x[..., :half], x[..., half:])


def both_halves(own, other):
    return jnp.where(
        lax.axis_index("head") == 0,
        jnp.concatenate([own, other], axis=-1),
        jnp.concatenate([other, own], axis=-1),
    )


def to_runs(blocks):
    count, me = lax.axis_size("ctx"), lax.axis_index("ctx")
    even = me % 2 == 0
    first = jnp.where(even, blocks[0], blocks[1])
    second = jnp.where(even, blocks[1], blocks[0])
    half = count // 2
    one = [(2 * j, j) for j in range(half)] + [(2 * j + 1, half + j) for j in range(half)]
    two = [(2 * j + 1, j) for j in range(half)] + [(2 * j, half + j) for j in range(half)]
    got_one = lax.ppermute(first, "ctx", one)
    got_two = lax.ppermute(second, "ctx", two)
    early = me < half
    return jnp.stack([jnp.where(early, got_one, got_two), jnp.where(early, got_two, got_one)])


def from_runs(blocks):
    count, me = lax.axis_size("ctx"), lax.axis_index("ctx")
    half = count // 2
    early = me < half
    one = [(j, 2 * j) for j in range(half)] + [(half + j, 2 * j + 1) for j in range(half)]
    two = [(j, 2 * j + 1) for j in range(half)] + [(half + j, 2 * j) for j in range(half)]
    got_one = lax.ppermute(jnp.where(early, blocks[0], blocks[1]), "ctx", one)
    got_two = lax.ppermute(jnp.where(early, blocks[1], blocks[0]), "ctx", two)
    even = me % 2 == 0
    return jnp.stack([jnp.where(even, got_one, got_two), jnp.where(even, got_two, got_one)])


def shared(move, blocks, extra=None):
    rows = blocks.shape[1] // 2
    mine = lax.axis_index("head")
    send = lax.dynamic_slice_in_dim(blocks, mine * rows, rows, 1)
    if extra is not None:
        send = jnp.concatenate([send, extra], axis=1)
    got = move(send)
    own = got[:, :rows]
    other = swap(own, "head", 1)
    whole = jnp.where(
        mine == 0,
        jnp.concatenate([own, other], axis=1),
        jnp.concatenate([other, own], axis=1),
    )
    return whole if extra is None else (whole, got[:, rows:])


def chain_shift(x, by):
    count = lax.axis_size("ctx")
    half = count // 2
    pairs = [
        (i, i + by) for i in range(count) if 0 <= i + by < count and i // half == (i + by) // half
    ]
    return lax.ppermute(x, "ctx", pairs)


def chain_scan(state, total, back):
    sign = -1 if back else 1
    half = lax.axis_size("ctx") // 2
    state = chain_shift(state, sign)
    if half == 2:
        return state
    total = chain_shift(total, sign)
    state = state.astype(F32)
    by = 1
    while by < half - 1:
        state = state + total * chain_shift(state, sign * by)
        total = total * chain_shift(total, sign * by)
        by *= 2
    return state.astype(BF16)


def shape(rows, cols, kind=F32):
    return jax.ShapeDtypeStruct((rows, cols), kind)


def layer_forward(residual, weights, small, common):
    wx, wstate, wgate, wout = weights
    info, segrow, _, spread = common
    count = residual.shape[0]
    width = spread.shape[1]
    wide = width + 2 * LANES
    root = lax.rsqrt(jnp.mean(residual * residual, axis=-1, keepdims=True) + EPSILON)
    normed = (residual * root * small["norm_gain"]).astype(BF16)
    both = mm(normed, wx)
    sraw = both_halves(both[:, width : width + LANES], mm(normed, wstate)).astype(BF16)
    raw = jnp.concatenate([both[:, :width].astype(BF16), sraw], axis=1)
    traw = both[:, width + LANES :]
    halo = chain_shift(raw[count - RIM :], 1)
    gate = mm(normed, wgate)
    act, delta, acc, state, total = kernel_call(
        conv_body,
        (
            shape(count, wide, BF16),
            shape(count, LANES),
            shape(count, LANES),
            shape(LANES, width),
            shape(8, LANES),
        ),
        [pltpu.VMEM((count + RIM, LANES), F32)],
        raw, halo, traw, info, small["taps"], small["perhead"], spread,
    )
    wide_total = jnp.repeat(total[0:1, : width // 64], 64, axis=1)
    start = chain_scan(state, wide_total, False)
    y, gated, squares, states = kernel_call(
        mix_body,
        (
            shape(count, width),
            shape(count, width),
            shape(count, LANES),
            shape(count, width, BF16),
        ),
        [pltpu.VMEM((LANES, width), F32)],
        act, delta, acc, info, segrow, small["perhead"], spread, start, gate, small["gate_gain"],
    )
    own = squares[:, 0:1]
    channels = width * lax.axis_size("head")
    out_root = lax.rsqrt((own + swap(own, "head", 1)) / channels + EPSILON)
    normal = (gated * out_root * small["gate_gain"][0:1]).astype(BF16)
    branch = mm(normal, wout, 1, 1)
    branch = branch + swap(branch, "head", 1)
    kept = (residual, root, normed, raw, traw, halo, gate, act, delta, acc, wide_total, y, normal)
    return residual + branch, kept + (states, out_root, branch)


def layer_backward(upstream, weights, small, common, kept):
    wx, _, wgate, wout = weights
    info, segrow, ahead, spread = common
    (
        residual, root, normed, raw, traw, halo, gate, act, delta, acc, wide_total, y, normal,
        states, out_root, branch,
    ) = kept
    count = residual.shape[0]
    width = spread.shape[1]
    wide = width + 2 * LANES
    channels = width * lax.axis_size("head")
    wire = upstream.astype(BF16)
    bn = mm(wire, wout)
    dot = jnp.sum(wire.astype(F32) * branch, axis=-1, keepdims=True)
    factor = jnp.concatenate(
        [out_root, out_root**2 * dot / channels, jnp.zeros((count, LANES - 2), F32)], axis=1
    )
    dy, dgate, gate_grad, local = kernel_call(
        gate_body,
        (
            shape(count, width, BF16),
            shape(count, width, BF16),
            shape(8, width),
            shape(LANES, width, BF16),
        ),
        [],
        bn, y, gate, small["gate_gain"], factor, act, acc, info, spread,
    )
    later = chain_scan(local, wide_total, True)
    out_grad = mm(wire, normal, 0, 0).astype(BF16)
    gate_w_grad = mm(normed, dgate, 0, 0).astype(BF16)
    back_gate = mm(dgate, wgate, 1, 1)
    dv, dvs, rim, last, dtraw, tap_grad, head_grad = kernel_call(
        back_body,
        (
            shape(count, width, BF16),
            shape(RIM + count, wide - width),
            shape(RIM, width),
            shape(RIM, width),
            shape(count, LANES, BF16),
            shape(8, wide),
            shape(8, LANES),
        ),
        [
            pltpu.VMEM((LANES, width), F32),
            pltpu.VMEM((count, wide), F32),
            pltpu.VMEM((count + RIM, LANES), F32),
            pltpu.VMEM((count + 2 * RIM, LANES), F32),
        ],
        act, delta, acc, traw, info, segrow, ahead, small["perhead"], spread,
        states, later, dy, raw, halo, small["taps"],
    )
    state = own_half(dvs) + swap(own_half(dvs, True), "head", 1)
    joined = chain_shift(jnp.concatenate([rim, state[:RIM]], axis=1), -1)
    state = state[RIM:] + jnp.pad(joined[:, width:], ((count - RIM, 0), (0, 0)))
    dv = lax.dynamic_update_slice_in_dim(
        dv, (last + joined[:, :width]).astype(BF16), count - RIM, 0
    )
    narrow = jnp.concatenate([dv, state.astype(BF16), dtraw], axis=1)
    x_grad = mm(normed, narrow, 0, 0).astype(BF16)
    back_normed = head_sum(back_gate + mm(narrow, wx, 1, 1))
    e = back_normed * small["norm_gain"]
    norm_grad = jnp.sum(back_normed * residual * root, axis=0)
    features = residual.shape[1]
    upstream = (
        upstream
        + root * e
        - residual * (root**3 * jnp.sum(e * residual, axis=-1, keepdims=True) / features)
    )
    return upstream, (x_grad, gate_w_grad, out_grad), (norm_grad, tap_grad, head_grad, gate_grad)


def pad_lanes(x, size):
    return jnp.pad(x, [(0, 0)] * (x.ndim - 1) + [(0, size - x.shape[-1])])


def pad_rows(x, size=8):
    return jnp.pad(x, ((0, size - x.shape[0]), (0, 0)))


def on_device(
    tokens, segments, cotangent, inner_proj, state_proj, step_proj, out_proj, norm_gain,
    mix_kernel, mix_bias, state_kernel, state_bias, step_bias, decay_log, skip_gain, gate_gain,
):
    layers = inner_proj.shape[0]
    features = tokens.shape[2]
    width = inner_proj.shape[3]
    heads = step_proj.shape[2]
    states = state_proj.shape[2]
    wide = width + states
    count = 2 * segments.shape[1]
    ctx, here = lax.axis_size("ctx"), lax.axis_index("ctx")
    me = lax.axis_index("dp") * ctx + here

    parts = []
    for layer in range(layers):
        parts.append(
            jnp.concatenate(
                [
                    inner_proj[layer, :, 1],
                    own_half(state_proj[layer]),
                    pad_lanes(step_proj[layer], LANES),
                ],
                axis=1,
            )
        )
        parts.append(jnp.concatenate([inner_proj[layer, :, 0], out_proj[layer].T], axis=1))
    gathered = []
    near = None
    for part in parts:
        if near is not None:
            part, near = lax.optimization_barrier((part, near))
            gathered.append(gather_far(near))
        near = gather_near(part)
    gathered.append(gather_far(near))
    weights = []
    for layer in range(layers):
        wx, rest = gathered[2 * layer : 2 * layer + 2]
        wstate = swap(wx[:, width : width + LANES], "head", 1)
        weights.append((wx, wstate, rest[:, :width], rest[:, width:]))

    block = features // (lax.axis_size("dp") * ctx)
    at = lax.broadcasted_iota(jnp.int32, (features, features), 0)
    to = lax.broadcasted_iota(jnp.int32, (features, features), 1)
    place = to // block
    owner = place // ctx * ctx
    steps = ctx.bit_length() - 1
    for k in range(steps):
        owner = owner + ((place >> k) & 1) * (1 << (steps - 1 - k))
    order = (at == (owner ^ me) * block + to % block).astype(BF16)

    def enter(blocks, extra=None):
        run = shared(to_runs, blocks, extra)
        run, extra = (run, None) if extra is None else run
        run = mm(run.reshape(count, features), order)
        return run if extra is None else (run, extra)

    def leave(run):
        run = mm(run.astype(BF16), order, 1, 1).astype(BF16)
        return shared(from_runs, run.reshape(2, count // 2, features))

    labels = jnp.zeros((2, 16, features), BF16)
    labels = labels.at[:, 0, : count // 2].set(segments.astype(BF16))
    residual, labels = enter(tokens, labels)
    seg = labels[:, 0, : count // 2].astype(F32).reshape(count)
    known = jnp.concatenate([chain_shift(seg[count - RIM :], 1), seg])
    chunked = seg.reshape(-1, CHUNK)
    chunk_before = known[RIM - 1 : RIM - 1 + count].reshape(-1, CHUNK)[:, :1]
    flags = [
        seg,
        known[RIM - 1 : -1] == seg,
        known[RIM - 2 : -2] == seg,
        known[RIM - 3 : -3] == seg,
        (chunked == chunk_before).reshape(-1),
        (chunked == chunked[:, -1:]).reshape(-1),
        seg == known[RIM - 1],
        seg == seg[-1],
    ]
    info = pad_lanes(jnp.stack([flag.astype(F32) for flag in flags], axis=1), LANES)
    segrow = jnp.broadcast_to(seg[None], (8, count))
    beyond = jnp.pad(known, (0, 3), constant_values=-1)
    ahead = pad_lanes(
        jnp.stack(
            [(beyond[d : d + count + RIM] == known).astype(F32) for d in range(4)], axis=1
        ),
        LANES,
    )
    at = lax.broadcasted_iota(jnp.int32, (LANES, width), 0)
    to = lax.broadcasted_iota(jnp.int32, (LANES, width), 1)
    spread = (at == to // (width // heads)).astype(BF16)
    common = (info, segrow, ahead, spread)

    gains = mm(norm_gain, order.astype(F32), precision=HIGH)
    smalls = []
    for layer in range(layers):
        taps = jnp.concatenate(
            [
                jnp.concatenate([mix_kernel[layer], state_kernel[layer]], axis=1),
                jnp.concatenate([mix_bias[layer], state_bias[layer]])[None],
            ]
        )
        perhead = jnp.stack([step_bias[layer], decay_log[layer], skip_gain[layer]])
        smalls.append(
            {
                "norm_gain": gains[layer],
                "taps": pad_rows(taps),
                "perhead": pad_rows(pad_lanes(perhead, LANES)),
                "gate_gain": jnp.broadcast_to(gate_gain[layer][None], (8, width)),
            }
        )

    saved = []
    for layer in range(layers):
        residual, kept = layer_forward(residual, weights[layer], smalls[layer], common)
        saved.append(kept)
        if layer == 0:
            cotangent, residual = lax.optimization_barrier((cotangent, residual))
            upstream = enter(cotangent)
    mixed = leave(residual)
    shards = [None] * layers
    others = [None] * layers
    for layer in reversed(range(layers)):
        upstream, matrices, (norm_grad, tap_grad, head_grad, gate_grad) = layer_backward(
            upstream, weights[layer], smalls[layer], common, saved[layer]
        )
        x_grad, gate_w_grad, out_grad = matrices
        shards[layer] = (scatter_rows(gate_w_grad, out_grad), scatter_rows(x_grad))
        norm_grad = mm(norm_grad[None], order.astype(F32), 1, 1, precision=HIGH)
        shared_taps = tap_grad[:, width:]
        shared_taps = shared_taps + swap(shared_taps, "head", 1)
        others[layer] = jnp.concatenate(
            [
                norm_grad.reshape(-1),
                gate_grad[0],
                tap_grad[:5, :width].reshape(-1),
                shared_taps[:5].reshape(-1),
                head_grad[:3].reshape(-1),
            ]
        ).reshape(-1, LANES)
    others = total_over(jnp.stack(others)).reshape(layers, -1)
    token_grad = leave(upstream)

    grads = [[], [], [], []]
    sums = [[] for _ in range(9)]
    for layer in range(layers):
        rest, x_shard = shards[layer]
        state_shard = x_shard[:, width : width + LANES]
        grads[0].append(jnp.stack([rest[:, :width], x_shard[:, :width]], axis=1))
        grads[1].append(both_halves(state_shard, swap(state_shard, "head", 1)))
        grads[2].append(x_shard[:, width + LANES : width + LANES + heads])
        grads[3].append(rest[:, width:].T)
        flat = others[layer]
        cut = 0
        pieces = []
        for size in (features, width, 5 * width, 5 * states, 3 * LANES):
            pieces.append(flat[cut : cut + size])
            cut += size
        taps = pieces[2].reshape(5, width)
        shared_taps = pieces[3].reshape(5, states)
        per = pieces[4].reshape(3, LANES)[:, :heads]
        for index, value in enumerate(
            (
                pieces[0], taps[:4], taps[4], shared_taps[:4], shared_taps[4],
                per[0], per[1], per[2], pieces[1],
            )
        ):
            sums[index].append(value)
    return (mixed, token_grad) + tuple(jnp.stack(v) for v in grads) + tuple(
        jnp.stack(v) for v in sums
    )


def solution(mesh):
    return jax.shard_map(
        on_device,
        mesh=mesh,
        in_specs=(
            P("dp", "ctx", None),
            P("dp", "ctx"),
            P("dp", "ctx", None),
            P(None, ("dp", "ctx"), None, "head"),
            P(None, ("dp", "ctx"), None),
            P(None, ("dp", "ctx"), "head"),
            P(None, "head", ("dp", "ctx")),
            P(),
            P(None, None, "head"),
            P(None, "head"),
            P(),
            P(),
            P(None, "head"),
            P(None, "head"),
            P(None, "head"),
            P(None, "head"),
        ),
        out_specs=(
            P("dp", "ctx", None),
            P("dp", "ctx", None),
            P(None, ("dp", "ctx"), None, "head"),
            P(None, ("dp", "ctx"), None),
            P(None, ("dp", "ctx"), "head"),
            P(None, "head", ("dp", "ctx")),
            P(),
            P(None, None, "head"),
            P(None, "head"),
            P(),
            P(),
            P(None, "head"),
            P(None, "head"),
            P(None, "head"),
            P(None, "head"),
        ),
        check_vma=False,
    )
```

time: 2060 us -> 641 us (0.31)
  waiting for transfers between devices: 1210 us -> 243 us
  blocking collectives: 265 us -> 0 us
  matrix products: 193 us -> 54.6 us
  local copies, waits for them, and re-layouts: 168 us -> 49.4 us
  starting transfers between devices: 15.9 us -> 123 us
  other arithmetic: 170 us -> 65.7 us
  Pallas kernels: 0 us -> 92.6 us
    reduce_scatter x2 -> x0, waiting for transfers between devices: 378 us -> none  [the longest x1 295 us: on_device(): lax.psum_scatter(stacked_inner, ('dp', 'ctx'), scatter_dimension=1, tiled...]
    all_gather x8 -> x0, waiting for transfers between devices: 359 us -> none  [the longest x4 261 us: entering(): pieces = jax.tree.map(lambda part: lax.all_gather(part, axis), value)]
    unnamed x20 -> x0, waiting for transfers between devices: 273 us -> none
    ppermute x5 -> x87, waiting for transfers between devices: 8.71 us -> 243 us  [the longest x70 211 us: swap(): return lax.ppermute(x, axis, [(i, i ^ bit) for i in range(size)])]
    all_gather x6 -> x0, blocking collectives: 206 us -> none  [the longest x2 92.3 us: on_device(): lax.all_gather(step_proj[layer], ('dp', 'ctx'), axis=0, tiled=True)]
    psum x6 -> x0, waiting for transfers between devices: 186 us -> none  [the longest x1 119 us: on_device(): lax.psum((norm_all, spread(kernel_all[..., :width]), spread(bias_all[...,...]
    dot_general x70 -> x27, matrix products: 193 us -> 54.6 us  [mm(): lax.dot_general(a, b, (((ca,), (cb,)), ((), ())), precision=precision, pr...]
    ppermute x5 -> x87, starting transfers between devices: 15 us -> 123 us  [the longest x70 64.9 us: swap(): return lax.ppermute(x, axis, [(i, i ^ bit) for i in range(size)])]
  transfers between devices with their start and end apart: 23 -> 87, of which waited for: 19 -> 34; matrix products, arithmetic and copies ran while one was open for 8% -> 21% of each run, Pallas kernels for 0% -> 12%
where the time goes in v1:
time: 641 us; the launch traced here: 633 us
  waiting for transfers between devices  243 us (38%)
  starting transfers between devices  123 us (19%)
  Pallas kernels  92.6 us (14%)
  other arithmetic  65.7 us (10%)
  matrix products  54.6 us (9%)
  local copies, waits for them, and re-layouts  49.4 us (8%)
    ppermute x70, waiting for transfers between devices, swap(): return lax.ppermute(x, axis, [(i, i ^ bit) for i in range(size)])  211 us
    pallas_call x8, Pallas kernels, kernel_call(): pl.pallas_call(body, out_shape=outs, scratch_shapes=scratch, compiler_par...  92.6 us
    ppermute x70, starting transfers between devices, swap(): return lax.ppermute(x, axis, [(i, i ^ bit) for i in range(size)])  64.9 us
    dot_general x27, matrix products, mm(): lax.dot_general(a, b, (((ca,), (cb,)), ((), ())), precision=precision, pr...  54.6 us
    ppermute x9, starting transfers between devices, chain_shift(): return lax.ppermute(x, 'ctx', pairs)  35.7 us
    unnamed x311, local copies, waits for them, and re-layouts  22.6 us
    ppermute x9, waiting for transfers between devices, chain_shift(): return lax.ppermute(x, 'ctx', pairs)  21.8 us
  transfers between devices with their start and end apart: 87, of which 34 were waited for; matrix products, arithmetic and copies ran while one was open for 21% of the time, Pallas kernels for 12%

profile of v1, /device:TPU:0, one launch (start us, length us, event | category | flops | bytes accessed | tf_op | source)
XLA Modules:
  0.0 632.5 jit_solution(299421430506201464)
XLA Ops:
  17.4 11.2 %collective-permute-done.3 = bf16[64,1280]{1,0:T(8,128)(2,1)S(1)} collective-permute-done((bf16[64,1280]{1,0:T(8,128)(2,1)S(1)}, bf16[64,1280]{1,0:T(8,128)(2,1)S(1)}, u32[]{:S(2)}, u32[]{:S(2)}) %collective-permute-start.3) | collective-permute-done | bytes 163872 | tf_op jit(solution)/shard_map/ppermute | solution.py:375
  48.7 6.5 %collective-permute-done.13 = bf16[64,2048]{1,0:T(8,128)(2,1)} collective-permute-done((bf16[64,2048]{1,0:T(8,128)(2,1)S(1)}, bf16[64,2048]{1,0:T(8,128)(2,1)}, u32[]{:S(2)}, u32[]{:S(2)}) %collective-permute-start.13) | collective-permute-done | bytes 262176 | tf_op jit(solution)/shard_map/ppermute | solution.py:375
  77.6 5.6 collective-permute-done.21
  95.3 5.7 shard_map.271
  113.3 18.0 %collective-permute-done.17 = bf16[128,2048]{1,0:T(8,128)(2,1)S(1)} collective-permute-done((bf16[128,2048]{1,0:T(8,128)(2,1)S(1)}, bf16[128,2048]{1,0:T(8,128)(2,1)S(1)}, u32[]{:S(2)}, u32[]{:S(2)}) %collective-permute-start.17) | collective-permute-done | bytes 524320 | tf_op jit(solution)/shard_map/ppermute | solution.py:375
  137.3 10.2 %shard_map.272 = (f32[512,1024]{1,0:T(8,128)}, f32[512,1024]{1,0:T(8,128)}, f32[512,128]{1,0:T(8,128)S(1)}, bf16[512,1024]{1,0:T(8,128)(2,1)S(1)}) custom-call(bf16[512,1280]{1,0:T(8,128)(2,1)S(1)} %get-tuple-element.74.act_ref, f32[512,128]{1,0:T(8,128)S(1)} %get-tuple-element.75.delta_ref, f32[512,128]{1,0:T(8,128)S(1)} %get-tuple-element.76.acc_ref, ...), custom_call_target="tpu_custom_call" | custom-call | tf_op jit(solution)/shard_map/pallas_call | solution.py:37
  161.3 26.4 %collective-permute-done.25 = bf16[128,1280]{1,0:T(8,128)(2,1)S(1)} collective-permute-done((bf16[128,1280]{1,0:T(8,128)(2,1)S(1)}, bf16[128,1280]{1,0:T(8,128)(2,1)S(1)}, u32[]{:S(2)}, u32[]{:S(2)}) %collective-permute-start.25) | collective-permute-done | bytes 327712 | tf_op jit(solution)/shard_map/ppermute | solution.py:375
  194.3 6.7 %collective-permute-done.34 = bf16[128,2048]{1,0:T(8,128)(2,1)S(1)} collective-permute-done((bf16[128,2048]{1,0:T(8,128)(2,1)S(1)}, bf16[128,2048]{1,0:T(8,128)(2,1)S(1)}, u32[]{:S(2)}, u32[]{:S(2)}) %collective-permute-start.34) | collective-permute-done | bytes 524320 | tf_op jit(solution)/shard_map/ppermute | solution.py:375
  213.1 5.7 shard_map.273
  218.8 14.3 %collective-permute-start.29 = (f32[128,1024]{1,0:T(8,128)S(1)}, f32[128,1024]{1,0:T(8,128)S(1)}, u32[]{:S(2)}, u32[]{:S(2)}) collective-permute-start(f32[128,1024]{1,0:T(8,128)S(1)} %get-tuple-element.88), channel_id=1, source_target_pairs={{0,2},{4,6},{1,3},{5,7},{8,10},{12,14},{9,11},{13,15},{16,18},{20,... | collective-permute-start | bytes 1572872 | tf_op jit(solution)/shard_map/ppermute | solution.py:508
  236.0 10.2 %shard_map.274 = (f32[512,1024]{1,0:T(8,128)}, f32[512,1024]{1,0:T(8,128)}, f32[512,128]{1,0:T(8,128)S(1)}, bf16[512,1024]{1,0:T(8,128)(2,1)S(1)}) custom-call(bf16[512,1280]{1,0:T(8,128)(2,1)S(1)} %get-tuple-element.85.act_ref, f32[512,128]{1,0:T(8,128)S(1)} %get-tuple-element.86.delta_ref, f32[512,128]{1,0:T(8,128)S(1)} %get-tuple-element.87.acc_ref, ...), custom_call_target="tpu_custom_call" | custom-call | tf_op jit(solution)/shard_map/pallas_call | solution.py:37
  257.4 6.6 %collective-permute-done.42 = bf16[128,1024]{1,0:T(8,128)(2,1)} collective-permute-done((bf16[128,1024]{1,0:T(8,128)(2,1)S(1)}, bf16[128,1024]{1,0:T(8,128)(2,1)}, u32[]{:S(2)}, u32[]{:S(2)}) %collective-permute-start.42) | collective-permute-done | bytes 262176 | tf_op jit(solution)/shard_map/ppermute | solution.py:468
  285.0 5.1 shard_map.275
  298.5 8.5 %collective-permute-start.39 = (bf16[128,1024]{1,0:T(8,128)(2,1)S(1)}, bf16[128,1024]{1,0:T(8,128)(2,1)S(1)}, u32[]{:S(2)}, u32[]{:S(2)}) collective-permute-start(bf16[128,1024]{1,0:T(8,128)(2,1)S(1)} %get-tuple-element.245), channel_id=1, source_target_pairs={{0,2},{2,6},{4,0},{6,4},{1,3},{3,7},{5,1},{7,5},{8,10},{10,14},{12... | collective-permute-start | bytes 786440 | tf_op jit(solution)/shard_map/ppermute | solution.py:480
  312.1 10.5 %collective-permute-done.44.later_ref = bf16[128,1024]{1,0:T(8,128)(2,1)S(1)} collective-permute-done((bf16[128,1024]{1,0:T(8,128)(2,1)S(1)}, bf16[128,1024]{1,0:T(8,128)(2,1)S(1)}, u32[]{:S(2)}, u32[]{:S(2)}) %collective-permute-start.44) | collective-permute-done | bytes 262176 | tf_op jit(solution)/shard_map/ppermute | solution.py:508
  322.6 25.1 %shard_map.276 = (bf16[512,1024]{1,0:T(8,128)(2,1)S(1)}, f32[520,256]{1,0:T(8,128)S(1)}, f32[8,1024]{1,0:T(8,128)S(1)}, f32[8,1024]{1,0:T(8,128)S(1)}, bf16[512,...) custom-call(bf16[512,1280]{1,0:T(8,128)(2,1)} %copy-done.5, f32[512,128]{1,0:T(8,128)S(1)} %copy-done.18, ...), custom_call_target="tpu_custom_call" | custom-call | tf_op jit(solution)/shard_map/pallas_call | solution.py:37
  384.0 25.3 %collective-permute-done.74 = bf16[256,1280]{0,1:T(8,128)(2,1)S(1)} collective-permute-done((bf16[256,1280]{0,1:T(8,128)(2,1)S(1)}, bf16[256,1280]{0,1:T(8,128)(2,1)S(1)}, u32[]{:S(2)}, u32[]{:S(2)}) %collective-permute-start.74) | collective-permute-done | bytes 655392 | tf_op jit(solution)/shard_map/ppermute | solution.py:375
  424.8 5.3 shard_map.277
  443.0 25.2 %shard_map.278 = (bf16[512,1024]{1,0:T(8,128)(2,1)S(1)}, f32[520,256]{1,0:T(8,128)S(1)}, f32[8,1024]{1,0:T(8,128)S(1)}, f32[8,1024]{1,0:T(8,128)S(1)}, bf16[512,...) custom-call(bf16[512,1280]{1,0:T(8,128)(2,1)} %copy-done.4, f32[512,128]{1,0:T(8,128)S(1)} %copy-done.16, ...), custom_call_target="tpu_custom_call" | custom-call | tf_op jit(solution)/shard_map/pallas_call | solution.py:37
  470.4 17.6 %collective-permute-done.78 = bf16[64,1280]{0,1:T(8,128)(2,1)} collective-permute-done((bf16[64,1280]{0,1:T(8,128)(2,1)S(1)}, bf16[64,1280]{0,1:T(8,128)(2,1)}, u32[]{:S(2)}, u32[]{:S(2)}) %collective-permute-start.78) | collective-permute-done | bytes 163872 | tf_op jit(solution)/shard_map/ppermute | solution.py:375
  508.5 22.3 %collective-permute-done.61 = bf16[128,1280]{0,1:T(8,128)(2,1)S(1)} collective-permute-done((bf16[128,1280]{0,1:T(8,128)(2,1)S(1)}, bf16[128,1280]{0,1:T(8,128)(2,1)S(1)}, u32[]{:S(2)}, u32[]{:S(2)}) %collective-permute-start.61) | collective-permute-done | bytes 327712 | tf_op jit(solution)/shard_map/ppermute | solution.py:375
  535.2 13.2 %collective-permute-done.62 = bf16[256,1280]{0,1:T(8,128)(2,1)S(1)} collective-permute-done((bf16[256,1280]{0,1:T(8,128)(2,1)S(1)}, bf16[256,1280]{0,1:T(8,128)(2,1)S(1)}, u32[]{:S(2)}, u32[]{:S(2)}) %collective-permute-start.62) | collective-permute-done | bytes 655392 | tf_op jit(solution)/shard_map/ppermute | solution.py:375
  584.0 12.3 %collective-permute-done.66 = bf16[64,1280]{0,1:T(8,128)(2,1)} collective-permute-done((bf16[64,1280]{0,1:T(8,128)(2,1)S(1)}, bf16[64,1280]{0,1:T(8,128)(2,1)}, u32[]{:S(2)}, u32[]{:S(2)}) %collective-permute-start.66) | collective-permute-done | bytes 163872 | tf_op jit(solution)/shard_map/ppermute | solution.py:375
  601.3 23.9 %collective-permute-done.60 = bf16[64,2048]{0,1:T(8,128)(2,1)S(1)} collective-permute-done((bf16[64,2048]{0,1:T(8,128)(2,1)S(1)}, bf16[64,2048]{0,1:T(8,128)(2,1)S(1)}, u32[]{:S(2)}, u32[]{:S(2)}) %collective-permute-start.60) | collective-permute-done | bytes 262176 | tf_op jit(solution)/shard_map/ppermute | solution.py:375
  (741 shorter events, 307.1 us)
Async XLA Ops:
  69.9 39.7 %collective-permute-start.16 = (bf16[256,2048]{1,0:T(8,128)(2,1)S(1)}, bf16[256,2048]{1,0:T(8,128)(2,1)S(1)}, u32[]{:S(2)}, u32[]{:S(2)}) collective-permute-start(bf16[256,2048]{1,0:T(8,128)(2,1)S(1)} %pad_maximum_fusion.5), channel_id=1, source_target_pairs={{0,16},{8,24},{16,0},{24,8},{1,17},{9,25},{17,1},{25,9},{2,18},{10... | collective-permute-start | bytes 3145736 | tf_op jit(solution)/shard_map/ppermute | solution.py:375
  71.5 35.0 %collective-permute-start.15 = (bf16[256,2048]{1,0:T(8,128)(2,1)S(1)}, bf16[256,2048]{1,0:T(8,128)(2,1)S(1)}, u32[]{:S(2)}, u32[]{:S(2)}) collective-permute-start(bf16[256,2048]{1,0:T(8,128)(2,1)S(1)} %pad_maximum_fusion.5), channel_id=1, source_target_pairs={{0,8},{8,0},{16,24},{24,16},{1,9},{9,1},{17,25},{25,17},{2,10},{10... | collective-permute-start | bytes 3145736 | tf_op jit(solution)/shard_map/ppermute | solution.py:375
  101.0 36.3 %collective-permute-start.12 = (f32[128,1024]{1,0:T(8,128)S(1)}, f32[128,1024]{1,0:T(8,128)S(1)}, u32[]{:S(2)}, u32[]{:S(2)}) collective-permute-start(f32[128,1024]{1,0:T(8,128)S(1)} %get-tuple-element.77), channel_id=1, source_target_pairs={{0,2},{4,6},{1,3},{5,7},{8,10},{12,14},{9,11},{13,15},{16,18},{20,... | collective-permute-start | bytes 1572872 | tf_op jit(solution)/shard_map/ppermute | solution.py:508
  105.2 51.8 %collective-permute-start.24 = (bf16[256,1280]{1,0:T(8,128)(2,1)S(1)}, bf16[256,1280]{1,0:T(8,128)(2,1)S(1)}, u32[]{:S(2)}, u32[]{:S(2)}) collective-permute-start(bf16[256,1280]{1,0:T(8,128)(2,1)S(1)} %pad_maximum_fusion.8), channel_id=1, source_target_pairs={{0,16},{8,24},{16,0},{24,8},{1,17},{9,25},{17,1},{25,9},{2,18},{10... | collective-permute-start | bytes 1966088 | tf_op jit(solution)/shard_map/ppermute | solution.py:375
  106.5 52.1 %collective-permute-start.23 = (bf16[256,1280]{1,0:T(8,128)(2,1)S(1)}, bf16[256,1280]{1,0:T(8,128)(2,1)}, u32[]{:S(2)}, u32[]{:S(2)}) collective-permute-start(bf16[256,1280]{1,0:T(8,128)(2,1)S(1)} %pad_maximum_fusion.8), channel_id=1, source_target_pairs={{0,8},{8,0},{16,24},{24,16},{1,9},{9,1},{17,25},{25,17},{2,10},{10... | collective-permute-start | bytes 1966088 | tf_op jit(solution)/shard_map/ppermute | solution.py:375
  153.4 48.4 %collective-permute-start.20 = (f32[512,1024]{1,0:T(8,128)S(1)}, f32[512,1024]{1,0:T(8,128)S(1)}, u32[]{:S(2)}, u32[]{:S(2)}) collective-permute-start(f32[512,1024]{1,0:T(8,128)S(1)} %fusion.27), channel_id=1, source_target_pairs={{0,1},{1,0},{2,3},{3,2},{4,5},{5,4},{6,7},{7,6},{8,9},{9,8},{10,11... | collective-permute-start | bytes 6291464 | tf_op jit(solution)/shard_map/ppermute | solution.py:375
  155.3 34.3 %collective-permute-start.33 = (bf16[256,2048]{1,0:T(8,128)(2,1)}, bf16[256,2048]{1,0:T(8,128)(2,1)S(1)}, u32[]{:S(2)}, u32[]{:S(2)}) collective-permute-start(bf16[256,2048]{1,0:T(8,128)(2,1)} %get-tuple-element.260), channel_id=1, source_target_pairs={{0,16},{8,24},{16,0},{24,8},{1,17},{9,25},{17,1},{25,9},{2,18},{10... | collective-permute-start | bytes 3145736 | tf_op jit(solution)/shard_map/ppermute | solution.py:375
  190.6 42.6 %collective-permute-start.35 = (bf16[128,2048]{1,0:T(8,128)(2,1)}, bf16[128,2048]{1,0:T(8,128)(2,1)S(1)}, u32[]{:S(2)}, u32[]{:S(2)}) collective-permute-start(bf16[128,2048]{1,0:T(8,128)(2,1)} %slice.847), channel_id=1, source_target_pairs={{0,8},{8,0},{16,24},{24,16},{1,9},{9,1},{17,25},{25,17},{2,10},{10... | collective-permute-start | bytes 1572872 | tf_op jit(solution)/shard_map/ppermute | solution.py:375
  297.6 51.8 %collective-permute-start.38 = (bf16[128,1024]{1,0:T(8,128)(2,1)S(1)}, bf16[128,1024]{1,0:T(8,128)(2,1)S(1)}, u32[]{:S(2)}, u32[]{:S(2)}) collective-permute-start(bf16[128,1024]{1,0:T(8,128)(2,1)S(1)} %get-tuple-element.244), channel_id=1, source_target_pairs={{0,0},{2,4},{4,2},{6,6},{1,1},{3,5},{5,3},{7,7},{8,8},{10,12},{12,... | collective-permute-start | bytes 786440 | tf_op jit(solution)/shard_map/ppermute | solution.py:479
  298.5 51.0 %collective-permute-start.39 = (bf16[128,1024]{1,0:T(8,128)(2,1)S(1)}, bf16[128,1024]{1,0:T(8,128)(2,1)S(1)}, u32[]{:S(2)}, u32[]{:S(2)}) collective-permute-start(bf16[128,1024]{1,0:T(8,128)(2,1)S(1)} %get-tuple-element.245), channel_id=1, source_target_pairs={{0,2},{2,6},{4,0},{6,4},{1,3},{3,7},{5,1},{7,5},{8,10},{10,14},{12... | collective-permute-start | bytes 786440 | tf_op jit(solution)/shard_map/ppermute | solution.py:480
  309.3 58.5 %collective-permute-start.69 = (bf16[128,2048]{0,1:T(8,128)(2,1)}, bf16[128,2048]{0,1:T(8,128)(2,1)}, u32[]{:S(2)}, u32[]{:S(2)}) collective-permute-start(bf16[128,2048]{0,1:T(8,128)(2,1)} %pad_maximum_fusion.21), channel_id=1, source_target_pairs={{0,8},{8,0},{16,24},{24,16},{1,9},{9,1},{17,25},{25,17},{2,10},{10... | collective-permute-start | bytes 1572872 | tf_op jit(solution)/shard_map/ppermute | solution.py:375
  311.6 54.3 %collective-permute-start.67 = (bf16[128,2048]{0,1:T(8,128)(2,1)}, bf16[128,2048]{0,1:T(8,128)(2,1)}, u32[]{:S(2)}, u32[]{:S(2)}) collective-permute-start(bf16[128,2048]{0,1:T(8,128)(2,1)} %pad_maximum_fusion.20), channel_id=1, source_target_pairs={{0,16},{8,24},{16,0},{24,8},{1,17},{9,25},{17,1},{25,9},{2,18},{10... | collective-permute-start | bytes 1572872 | tf_op jit(solution)/shard_map/ppermute | solution.py:375
  367.2 45.2 %collective-permute-start.68 = (bf16[256,2048]{0,1:T(8,128)(2,1)S(1)}, bf16[256,2048]{0,1:T(8,128)(2,1)S(1)}, u32[]{:S(2)}, u32[]{:S(2)}) collective-permute-start(bf16[256,2048]{0,1:T(8,128)(2,1)S(1)} %add_convert_fusion.1), channel_id=1, source_target_pairs={{0,8},{8,0},{16,24},{24,16},{1,9},{9,1},{17,25},{25,17},{2,10},{10... | collective-permute-start | bytes 3145736 | tf_op jit(solution)/shard_map/ppermute | solution.py:375
  369.3 43.1 %collective-permute-start.70 = (bf16[256,2048]{0,1:T(8,128)(2,1)S(1)}, bf16[256,2048]{0,1:T(8,128)(2,1)S(1)}, u32[]{:S(2)}, u32[]{:S(2)}) collective-permute-start(bf16[256,2048]{0,1:T(8,128)(2,1)S(1)} %add_convert_fusion), channel_id=1, source_target_pairs={{0,16},{8,24},{16,0},{24,8},{1,17},{9,25},{17,1},{25,9},{2,18},{10... | collective-permute-start | bytes 3145736 | tf_op jit(solution)/shard_map/ppermute | solution.py:375
  375.4 33.9 %collective-permute-start.74 = (bf16[256,1280]{0,1:T(8,128)(2,1)S(1)}, bf16[256,1280]{0,1:T(8,128)(2,1)S(1)}, u32[]{:S(2)}, u32[]{:S(2)}) collective-permute-start(bf16[256,1280]{0,1:T(8,128)(2,1)S(1)} %get-tuple-element.212), channel_id=1, source_target_pairs={{0,8},{8,0},{16,24},{24,16},{1,9},{9,1},{17,25},{25,17},{2,10},{10... | collective-permute-start | bytes 1966088 | tf_op jit(solution)/shard_map/ppermute | solution.py:375
  381.3 34.5 %collective-permute-start.47 = (bf16[512,1024]{1,0:T(8,128)(2,1)S(1)}, bf16[512,1024]{1,0:T(8,128)(2,1)S(1)}, u32[]{:S(2)}, u32[]{:S(2)}) collective-permute-start(bf16[512,1024]{1,0:T(8,128)(2,1)S(1)} %add_convert_fusion.5), channel_id=1, source_target_pairs={{0,1},{1,0},{2,3},{3,2},{4,5},{5,4},{6,7},{7,6},{8,9},{9,8},{10,11... | collective-permute-start | bytes 3145736 | tf_op jit(solution)/shard_map/ppermute | solution.py:375
  412.4 55.9 %collective-permute-start.77 = (bf16[128,1280]{0,1:T(8,128)(2,1)}, bf16[128,1280]{0,1:T(8,128)(2,1)}, u32[]{:S(2)}, u32[]{:S(2)}) collective-permute-start(bf16[128,1280]{0,1:T(8,128)(2,1)} %slice.1074), channel_id=1, source_target_pairs={{0,2},{2,0},{4,6},{6,4},{1,3},{3,1},{5,7},{7,5},{8,10},{10,8},{12,... | collective-permute-start | bytes 983048 | tf_op jit(solution)/shard_map/ppermute | solution.py:375
  413.8 77.2 %collective-permute-start.71 = (bf16[128,2048]{0,1:T(8,128)(2,1)}, bf16[128,2048]{0,1:T(8,128)(2,1)}, u32[]{:S(2)}, u32[]{:S(2)}) collective-permute-start(bf16[128,2048]{0,1:T(8,128)(2,1)} %slice.1070), channel_id=1, source_target_pairs={{0,2},{2,0},{4,6},{6,4},{1,3},{3,1},{5,7},{7,5},{8,10},{10,8},{12,... | collective-permute-start | bytes 1572872 | tf_op jit(solution)/shard_map/ppermute | solution.py:375
  436.8 60.6 %collective-permute-start.57 = (bf16[128,2048]{0,1:T(8,128)(2,1)}, bf16[128,2048]{0,1:T(8,128)(2,1)}, u32[]{:S(2)}, u32[]{:S(2)}) collective-permute-start(bf16[128,2048]{0,1:T(8,128)(2,1)} %pad_maximum_fusion.19), channel_id=1, source_target_pairs={{0,8},{8,0},{16,24},{24,16},{1,9},{9,1},{17,25},{25,17},{2,10},{10... | collective-permute-start | bytes 1572872 | tf_op jit(solution)/shard_map/ppermute | solution.py:375
  439.1 53.4 %collective-permute-start.55 = (bf16[128,2048]{0,1:T(8,128)(2,1)}, bf16[128,2048]{0,1:T(8,128)(2,1)}, u32[]{:S(2)}, u32[]{:S(2)}) collective-permute-start(bf16[128,2048]{0,1:T(8,128)(2,1)} %pad_maximum_fusion.18), channel_id=1, source_target_pairs={{0,16},{8,24},{16,0},{24,8},{1,17},{9,25},{17,1},{25,9},{2,18},{10... | collective-permute-start | bytes 1572872 | tf_op jit(solution)/shard_map/ppermute | solution.py:375
  492.4 39.8 %collective-permute-start.72 = (bf16[64,2048]{0,1:T(8,128)(2,1)S(1)}, bf16[64,2048]{0,1:T(8,128)(2,1)S(1)}, u32[]{:S(2)}, u32[]{:S(2)}) collective-permute-start(bf16[64,2048]{0,1:T(8,128)(2,1)S(1)} %slice.1069), channel_id=1, source_target_pairs={{0,4},{2,6},{4,0},{6,2},{1,5},{3,7},{5,1},{7,3},{8,12},{10,14},{12... | collective-permute-start | bytes 786440 | tf_op jit(solution)/shard_map/ppermute | solution.py:375
  493.9 74.1 %collective-permute-start.56 = (bf16[256,2048]{0,1:T(8,128)(2,1)S(1)}, bf16[256,2048]{0,1:T(8,128)(2,1)S(1)}, u32[]{:S(2)}, u32[]{:S(2)}) collective-permute-start(bf16[256,2048]{0,1:T(8,128)(2,1)S(1)} %add_convert_fusion.3), channel_id=1, source_target_pairs={{0,8},{8,0},{16,24},{24,16},{1,9},{9,1},{17,25},{25,17},{2,10},{10... | collective-permute-start | bytes 3145736 | tf_op jit(solution)/shard_map/ppermute | solution.py:375
  498.8 70.2 %collective-permute-start.58 = (bf16[256,2048]{0,1:T(8,128)(2,1)S(1)}, bf16[256,2048]{0,1:T(8,128)(2,1)S(1)}, u32[]{:S(2)}, u32[]{:S(2)}) collective-permute-start(bf16[256,2048]{0,1:T(8,128)(2,1)S(1)} %add_convert_fusion.2), channel_id=1, source_target_pairs={{0,16},{8,24},{16,0},{24,8},{1,17},{9,25},{17,1},{25,9},{2,18},{10... | collective-permute-start | bytes 3145736 | tf_op jit(solution)/shard_map/ppermute | solution.py:375
  578.2 51.3 %collective-permute-start.54 = (bf16[2,128,1024]{2,1,0:T(8,128)(2,1)}, bf16[2,128,1024]{2,1,0:T(8,128)(2,1)}, u32[]{:S(2)}, u32[]{:S(2)}) collective-permute-start(bf16[2,128,1024]{2,1,0:T(8,128)(2,1)} %pad_maximum_fusion.17), channel_id=1, source_target_pairs={{0,1},{1,0},{2,3},{3,2},{4,5},{5,4},{6,7},{7,6},{8,9},{9,8},{10,11... | collective-permute-start | bytes 1572872 | tf_op jit(solution)/shard_map/ppermute | solution.py:375
  (201 other events, 2665.5 us)

commit v2 on v1

--- a/solution.py
+++ b/solution.py
@@ -380,26 +380,39 @@
     return [1 << k for k in reversed(range(size.bit_length() - 1))]
 
 
-def gather_near(x):
-    for bit in bits_of("ctx"):
-        x = jnp.concatenate([x, swap(x, "ctx", bit)], axis=0)
-    return x
-
-
-def gather_far(near):
-    if lax.axis_size("dp") != 4:
-        x = near
-        for bit in reversed(bits_of("dp")):
-            x = jnp.concatenate([x, swap(x, "dp", bit)], axis=0)
-        return x
-    half = near.shape[0] // 2
-    one = swap(near, "dp", 1)
-    two = swap(near, "dp", 2)
-    three = [swap(one[:half], "dp", 2), swap(two[half:], "dp", 1)]
-    return jnp.concatenate([near, one, two] + three, axis=0)
-
-
-def scatter_rows(*matrices):
+def after(value, *ties):
+    ties = [tie for tie in ties if tie is not None]
+    return lax.optimization_barrier((value, ties))[0] if ties else value
+
+
+def gather_all(parts, follow):
+    wholes = []
+    four = lax.axis_size("dp") == 4
+    near_before = cross_before = None
+    for index, part in enumerate(parts):
+        near = after(part, near_before)
+        for bit in bits_of("ctx"):
+            near = jnp.concatenate([near, swap(near, "ctx", bit)], axis=0)
+        if index == 0:
+            follow(near)
+        near_before = near
+        near = after(near, cross_before)
+        if not four:
+            for bit in reversed(bits_of("dp")):
+                near = jnp.concatenate([near, swap(near, "dp", bit)], axis=0)
+            cross_before = near
+            wholes.append(near)
+            continue
+        half = near.shape[0] // 2
+        one = swap(near, "dp", 1)
+        two = swap(near, "dp", 2)
+        three = [swap(one[:half], "dp", 2), swap(two[half:], "dp", 1)]
+        cross_before = three if index % 2 == 0 and index > 0 else (one, two)
+        wholes.append(jnp.concatenate([near, one, two] + three, axis=0))
+    return wholes
+
+
+def scatter_steps(*matrices):
     count = lax.axis_size("dp")
     group = matrices[0].shape[0] // count
 
@@ -407,33 +420,61 @@
         return jnp.concatenate([g[start : start + size] for g in matrices], axis=1)
 
     if count != 4:
-        whole = part(0, count * group).astype(F32)
+        near = part(0, count * group).astype(F32)
         for bit in bits_of("dp"):
             size = bit * group
-            whole = whole[:size] + swap(whole[size:].astype(BF16), "dp", bit).astype(F32)
-        near = whole
+            got = swap(near[size:].astype(BF16), "dp", bit)
+            got = yield got
+            near = near[:size] + got.astype(F32)
     else:
         half = group // 2
-        far_one = swap(part(3 * group, half), "dp", 2).astype(F32)
-        far_two = swap(part(3 * group + half, half), "dp", 1).astype(F32)
-        none = jnp.zeros_like(far_one)
-        one = part(group, group).astype(F32) + jnp.concatenate([far_one, none])
-        two = part(2 * group, group).astype(F32) + jnp.concatenate([none, far_two])
-        near = (
-            part(0, group).astype(F32)
-            + swap(one.astype(BF16), "dp", 1).astype(F32)
-            + swap(two.astype(BF16), "dp", 2).astype(F32)
-        )
+        far = (
+            swap(part(3 * group, half), "dp", 2),
+            swap(part(3 * group + half, half), "dp", 1),
+        )
+        far = yield far
+        none = jnp.zeros(far[0].shape, F32)
+        one = part(group, group).astype(F32) + jnp.concatenate([far[0].astype(F32), none])
+        two = part(2 * group, group).astype(F32) + jnp.concatenate([none, far[1].astype(F32)])
+        got = (swap(one.astype(BF16), "dp", 1), swap(two.astype(BF16), "dp", 2))
+        got = yield got
+        near = part(0, group).astype(F32) + got[0].astype(F32) + got[1].astype(F32)
     for bit in reversed(bits_of("ctx")):
         half = near.shape[0] // 2
-        near = near[:half] + swap(near[half:].astype(BF16), "ctx", bit).astype(F32)
+        got = swap(near[half:].astype(BF16), "ctx", bit)
+        got = yield got
+        near = near[:half] + got.astype(F32)
     return near
 
 
-def total_over(x):
-    for axis in ("ctx", "dp"):
-        for bit in bits_of(axis):
-            x = x + swap(x, axis, bit)
+class Scatter:
+    def __init__(self, steps):
+        self.steps = steps
+        self.result = None
+        self.flying = next(self.steps)
+
+    def step(self, got):
+        try:
+            self.flying = self.steps.send(got)
+        except StopIteration as stop:
+            self.result = stop.value
+
+
+def advance(scatters, value):
+    scatters = [scatter for scatter in scatters if scatter.result is None]
+    if scatters:
+        flying = [scatter.flying for scatter in scatters]
+        value, flying = lax.optimization_barrier((value, flying))
+        for scatter, got in zip(scatters, flying):
+            scatter.step(got)
+    return value
+
+
+def total_steps(x):
+    for axis in ("dp", "ctx"):
+        for bit in reversed(bits_of(axis)):
+            got = yield swap(x, axis, bit)
+            x = x + got
     return x
 
 
@@ -577,7 +618,7 @@
     return residual + branch, kept + (states, out_root, branch)
 
 
-def layer_backward(upstream, weights, small, common, kept):
+def layer_backward(upstream, weights, small, common, kept, pending):
     wx, _, wgate, wout = weights
     info, segrow, ahead, spread = common
     (
@@ -608,6 +649,8 @@
     later = chain_scan(local, wide_total, True)
     out_grad = mm(wire, normal, 0, 0).astype(BF16)
     gate_w_grad = mm(normed, dgate, 0, 0).astype(BF16)
+    later = advance(pending, later)
+    rest = Scatter(scatter_steps(gate_w_grad, out_grad))
     back_gate = mm(dgate, wgate, 1, 1)
     dv, dvs, rim, last, dtraw, tap_grad, head_grad = kernel_call(
         back_body,
@@ -636,7 +679,9 @@
         dv, (last + joined[:, :width]).astype(BF16), count - RIM, 0
     )
     narrow = jnp.concatenate([dv, state.astype(BF16), dtraw], axis=1)
+    narrow = advance(pending + [rest], narrow)
     x_grad = mm(normed, narrow, 0, 0).astype(BF16)
+    pending = pending + [rest, Scatter(scatter_steps(x_grad))]
     back_normed = head_sum(back_gate + mm(narrow, wx, 1, 1))
     e = back_normed * small["norm_gain"]
     norm_grad = jnp.sum(back_normed * residual * root, axis=0)
@@ -646,7 +691,7 @@
         + root * e
         - residual * (root**3 * jnp.sum(e * residual, axis=-1, keepdims=True) / features)
     )
-    return upstream, (x_grad, gate_w_grad, out_grad), (norm_grad, tap_grad, head_grad, gate_grad)
+    return upstream, pending, (norm_grad, tap_grad, head_grad, gate_grad)
 
 
 def pad_lanes(x, size):
@@ -673,25 +718,15 @@
 
     parts = []
     for layer in range(layers):
-        parts.append(
-            jnp.concatenate(
-                [
-                    inner_proj[layer, :, 1],
-                    own_half(state_proj[layer]),
-                    pad_lanes(step_proj[layer], LANES),
-                ],
-                axis=1,
-            )
-        )
-        parts.append(jnp.concatenate([inner_proj[layer, :, 0], out_proj[layer].T], axis=1))
-    gathered = []
-    near = None
-    for part in parts:
-        if near is not None:
-            part, near = lax.optimization_barrier((part, near))
-            gathered.append(gather_far(near))
-        near = gather_near(part)
-    gathered.append(gather_far(near))
+        first = [
+            inner_proj[layer, :, 1],
+            own_half(state_proj[layer]),
+            pad_lanes(step_proj[layer], LANES),
+        ]
+        rest = [inner_proj[layer, :, 0], out_proj[layer].T]
+        parts.extend(jnp.concatenate(group, axis=1) for group in (first, rest))
+    began = []
+    gathered = gather_all(parts, began.append)
     weights = []
     for layer in range(layers):
         wx, rest = gathered[2 * layer : 2 * layer + 2]
@@ -718,11 +753,15 @@
         run = mm(run.astype(BF16), order, 1, 1).astype(BF16)
         return shared(from_runs, run.reshape(2, count // 2, features))
 
-    labels = jnp.zeros((2, 16, features), BF16)
-    labels = labels.at[:, 0, : count // 2].set(segments.astype(BF16))
-    residual, labels = enter(tokens, labels)
-    seg = labels[:, 0, : count // 2].astype(F32).reshape(count)
-    known = jnp.concatenate([chain_shift(seg[count - RIM :], 1), seg])
+    rows = count // 2
+    behind = [(i, i + 1) for i in range(ctx - 1)]
+    previous = lax.ppermute(after(segments, *began)[:, rows - RIM :], "ctx", behind)
+    labels = jnp.concatenate([segments, previous], axis=1).astype(BF16)
+    labels = jnp.pad(labels[:, None], ((0, 0), (0, 15), (0, features - rows - RIM)))
+    residual, labels = enter(after(tokens, *began), labels)
+    labels = labels[:, 0].astype(F32)
+    seg = labels[:, :rows].reshape(count)
+    known = jnp.concatenate([labels[0, rows : rows + RIM], seg])
     chunked = seg.reshape(-1, CHUNK)
     chunk_before = known[RIM - 1 : RIM - 1 + count].reshape(-1, CHUNK)[:, :1]
     flags = [
@@ -773,17 +812,16 @@
         residual, kept = layer_forward(residual, weights[layer], smalls[layer], common)
         saved.append(kept)
         if layer == 0:
-            cotangent, residual = lax.optimization_barrier((cotangent, residual))
+            cotangent = after(cotangent, gathered[0])
             upstream = enter(cotangent)
+            residual, upstream = lax.optimization_barrier((residual, upstream))
     mixed = leave(residual)
-    shards = [None] * layers
+    pending = []
     others = [None] * layers
     for layer in reversed(range(layers)):
-        upstream, matrices, (norm_grad, tap_grad, head_grad, gate_grad) = layer_backward(
-            upstream, weights[layer], smalls[layer], common, saved[layer]
-        )
-        x_grad, gate_w_grad, out_grad = matrices
-        shards[layer] = (scatter_rows(gate_w_grad, out_grad), scatter_rows(x_grad))
+        upstream, pending, (norm_grad, tap_grad, head_grad, gate_grad) = layer_backward(
+            upstream, weights[layer], smalls[layer], common, saved[layer], pending
+        )
         norm_grad = mm(norm_grad[None], order.astype(F32), 1, 1, precision=HIGH)
         shared_taps = tap_grad[:, width:]
         shared_taps = shared_taps + swap(shared_taps, "head", 1)
@@ -796,8 +834,13 @@
                 head_grad[:3].reshape(-1),
             ]
         ).reshape(-1, LANES)
-    others = total_over(jnp.stack(others)).reshape(layers, -1)
+    pending.append(Scatter(total_steps(jnp.stack(others))))
     token_grad = leave(upstream)
+    while any(scatter.result is None for scatter in pending):
+        advance(pending, ())
+    done = [scatter.result for scatter in pending]
+    others = done.pop().reshape(layers, -1)
+    shards = [done[2 * index : 2 * index + 2] for index in reversed(range(layers))]
 
     grads = [[], [], [], []]
     sums = [[] for _ in range(9)]

time: 641 us -> 576 us (0.90)
  waiting for transfers between devices: 243 us -> 187 us
  starting transfers between devices: 123 us -> 115 us
    ppermute x70, waiting for transfers between devices: 211 us -> 154 us  [swap(): return lax.ppermute(x, axis, [(i, i ^ bit) for i in range(size)])]
    ppermute x9 -> x8, starting transfers between devices: 35.7 us -> 24.2 us  [chain_shift(): return lax.ppermute(x, 'ctx', pairs)]
    ppermute x2, starting transfers between devices: 10.7 us -> 3.3 us  [from_runs(): got_two = lax.ppermute(jnp.where(early, blocks[1], blocks[0]), 'ctx', two)]
    unnamed x311 -> x339, local copies, waits for them, and re-layouts: 22.6 us -> 26.2 us
    ppermute x9 -> x8, waiting for transfers between devices: 21.8 us -> 18.5 us  [chain_shift(): return lax.ppermute(x, 'ctx', pairs)]
  transfers between devices with their start and end apart: 87 -> 87, of which waited for: 34 -> 30; matrix products, arithmetic and copies ran while one was open for 21% -> 22% of each run, Pallas kernels for 12% -> 14%
where the time goes in v2:
time: 576 us; the launch traced here: 566 us
  waiting for transfers between devices  187 us (32%)
  starting transfers between devices  115 us (20%)
  Pallas kernels  92.7 us (16%)
  other arithmetic  59.8 us (10%)
  local copies, waits for them, and re-layouts  53.8 us (9%)
  matrix products  53.3 us (9%)
    ppermute x70, waiting for transfers between devices, swap(): return lax.ppermute(x, axis, [(i, i ^ bit) for i in range(size)])  154 us
    pallas_call x8, Pallas kernels, kernel_call(): pl.pallas_call(body, out_shape=outs, scratch_shapes=scratch, compiler_par...  92.7 us
    ppermute x70, starting transfers between devices, swap(): return lax.ppermute(x, axis, [(i, i ^ bit) for i in range(size)])  67.1 us
    dot_general x27, matrix products, mm(): lax.dot_general(a, b, (((ca,), (cb,)), ((), ())), precision=precision, pr...  53.3 us
    unnamed x339, local copies, waits for them, and re-layouts  26.2 us
    ppermute x8, starting transfers between devices, chain_shift(): return lax.ppermute(x, 'ctx', pairs)  24.2 us
    ppermute x8, waiting for transfers between devices, chain_shift(): return lax.ppermute(x, 'ctx', pairs)  18.5 us
  transfers between devices with their start and end apart: 87, of which 30 were waited for; matrix products, arithmetic and copies ran while one was open for 22% of the time, Pallas kernels for 14%

profile of v2, /device:TPU:0, one launch (start us, length us, event | category | flops | bytes accessed | tf_op | source)
XLA Modules:
  0.0 565.8 jit_solution(10469732096003633323)
XLA Ops:
  22.4 7.1 %collective-permute-done.1 = bf16[128,1280]{1,0:T(8,128)(2,1)S(1)} collective-permute-done((bf16[128,1280]{1,0:T(8,128)(2,1)}, bf16[128,1280]{1,0:T(8,128)(2,1)S(1)}, u32[]{:S(2)}, u32[]{:S(2)}) %collective-permute-start.1) | collective-permute-done | bytes 327712 | tf_op jit(solution)/shard_map/ppermute | solution.py:375
  41.1 7.9 %collective-permute-start.4 = (bf16[144,1024]{1,0:T(8,128)(2,1)S(1)}, bf16[144,1024]{1,0:T(8,128)(2,1)S(1)}, u32[]{:S(2)}, u32[]{:S(2)}) collective-permute-start(bf16[144,1024]{1,0:T(8,128)(2,1)S(1)} %get-tuple-element.306), channel_id=1, source_target_pairs={{2,0},{6,2},{0,4},{4,6},{3,1},{7,3},{1,5},{5,7},{10,8},{14,10},{8,... | collective-permute-start | bytes 884744 | tf_op jit(solution)/shard_map/ppermute | solution.py:509
  68.2 9.0 %collective-permute-start.24 = (bf16[64,1280]{1,0:T(8,128)(2,1)S(1)}, bf16[64,1280]{1,0:T(8,128)(2,1)S(1)}, u32[]{:S(2)}, u32[]{:S(2)}) collective-permute-start(bf16[64,1280]{1,0:T(8,128)(2,1)S(1)} %fusion.50), channel_id=1, source_target_pairs={{0,4},{2,6},{4,0},{6,2},{1,5},{3,7},{5,1},{7,3},{8,12},{10,14},{12... | collective-permute-start | bytes 491528 | tf_op jit(solution)/shard_map/ppermute | solution.py:375
  92.5 7.5 %collective-permute-done.22 = bf16[128,1024]{1,0:T(8,128)(2,1)S(1)} collective-permute-done((bf16[128,1024]{1,0:T(8,128)(2,1)S(1)}, bf16[128,1024]{1,0:T(8,128)(2,1)S(1)}, u32[]{:S(2)}, u32[]{:S(2)}) %collective-permute-start.22) | collective-permute-done | bytes 262176 | tf_op jit(solution)/shard_map/ppermute | solution.py:509
  101.5 5.1 collective-permute-start.11
  108.0 5.7 %shard_map.271 = (bf16[512,1280]{1,0:T(8,128)(2,1)S(1)}, f32[512,128]{1,0:T(8,128)S(1)}, f32[512,128]{1,0:T(8,128)S(1)}, f32[128,1024]{1,0:T(8,128)S(1)}, f32[8,128]{1,0:T(8,128)}) custom-call(bf16[512,1280]{1,0:T(8,128)(2,1)S(1)} %pad_maximum_fusion.1.raw_ref, bf16[8,1280]{1,0:T(8,128)(2,1)S(1)} %collective-permute-done.11.halo_ref, ...), custom_call_target="tpu_custom_call" | custom-call | tf_op jit(solution)/shard_map/pallas_call | solution.py:37
  128.2 8.4 %collective-permute-done.17 = bf16[128,2048]{1,0:T(8,128)(2,1)S(1)} collective-permute-done((bf16[128,2048]{1,0:T(8,128)(2,1)S(1)}, bf16[128,2048]{1,0:T(8,128)(2,1)S(1)}, u32[]{:S(2)}, u32[]{:S(2)}) %collective-permute-start.17) | collective-permute-done | bytes 524320 | tf_op jit(solution)/shard_map/ppermute | solution.py:375
  143.6 10.2 %shard_map.272 = (f32[512,1024]{1,0:T(8,128)}, f32[512,1024]{1,0:T(8,128)}, f32[512,128]{1,0:T(8,128)S(1)}, bf16[512,1024]{1,0:T(8,128)(2,1)S(1)}) custom-call(bf16[512,1280]{1,0:T(8,128)(2,1)S(1)} %get-tuple-element.97.act_ref, f32[512,128]{1,0:T(8,128)S(1)} %get-tuple-element.98.delta_ref, f32[512,128]{1,0:T(8,128)S(1)} %get-tuple-element.99.acc_ref, ...), custom_call_target="tpu_custom_call" | custom-call | tf_op jit(solution)/shard_map/pallas_call | solution.py:37
  168.5 22.8 %collective-permute-done.35 = bf16[256,2048]{1,0:T(8,128)(2,1)S(1)} collective-permute-done((bf16[256,2048]{1,0:T(8,128)(2,1)S(1)}, bf16[256,2048]{1,0:T(8,128)(2,1)S(1)}, u32[]{:S(2)}, u32[]{:S(2)}) %collective-permute-start.35) | collective-permute-done | bytes 1048608 | tf_op jit(solution)/shard_map/ppermute | solution.py:375
  194.0 9.3 %collective-permute-done.37 = bf16[128,2048]{1,0:T(8,128)(2,1)S(1)} collective-permute-done((bf16[128,2048]{1,0:T(8,128)(2,1)S(1)}, bf16[128,2048]{1,0:T(8,128)(2,1)S(1)}, u32[]{:S(2)}, u32[]{:S(2)}) %collective-permute-start.37) | collective-permute-done | bytes 524320 | tf_op jit(solution)/shard_map/ppermute | solution.py:375
  215.5 5.7 %shard_map.273 = (bf16[512,1280]{1,0:T(8,128)(2,1)S(1)}, f32[512,128]{1,0:T(8,128)S(1)}, f32[512,128]{1,0:T(8,128)S(1)}, f32[128,1024]{1,0:T(8,128)S(1)}, f32[8,128]{1,0:T(8,128)}) custom-call(bf16[512,1280]{1,0:T(8,128)(2,1)S(1)} %pad_maximum_fusion.2.raw_ref, bf16[8,1280]{1,0:T(8,128)(2,1)S(1)} %collective-permute-done.31.halo_ref, ...), custom_call_target="tpu_custom_call" | custom-call | tf_op jit(solution)/shard_map/pallas_call | solution.py:37
  232.7 10.2 %shard_map.274 = (f32[512,1024]{1,0:T(8,128)}, f32[512,1024]{1,0:T(8,128)}, f32[512,128]{1,0:T(8,128)S(1)}, bf16[512,1024]{1,0:T(8,128)(2,1)S(1)}) custom-call(bf16[512,1280]{1,0:T(8,128)(2,1)S(1)} %get-tuple-element.109.act_ref, f32[512,128]{1,0:T(8,128)S(1)} %get-tuple-element.110.delta_ref, f32[512,128]{1,0:T(8,128)S(1)} %get-tuple-element.111.acc_ref, ...), custom_call_target="tpu_custom_call" | custom-call | tf_op jit(solution)/shard_map/pallas_call | solution.py:37
  264.4 5.1 shard_map.275
  289.1 25.2 %shard_map.276 = (bf16[512,1024]{1,0:T(8,128)(2,1)S(1)}, f32[520,256]{1,0:T(8,128)S(1)}, f32[8,1024]{1,0:T(8,128)S(1)}, f32[8,1024]{1,0:T(8,128)S(1)}, bf16[512,...) custom-call(bf16[512,1280]{1,0:T(8,128)(2,1)} %copy-done.6, f32[512,128]{1,0:T(8,128)S(1)} %copy-done.11, ...), custom_call_target="tpu_custom_call" | custom-call | tf_op jit(solution)/shard_map/pallas_call | solution.py:37
  358.4 5.3 shard_map.277
  373.7 25.2 %shard_map.278 = (bf16[512,1024]{1,0:T(8,128)(2,1)S(1)}, f32[520,256]{1,0:T(8,128)S(1)}, f32[8,1024]{1,0:T(8,128)S(1)}, f32[8,1024]{1,0:T(8,128)S(1)}, bf16[512,...) custom-call(bf16[512,1280]{1,0:T(8,128)(2,1)} %copy-done.4, f32[512,128]{1,0:T(8,128)S(1)} %copy-done.9, ...), custom_call_target="tpu_custom_call" | custom-call | tf_op jit(solution)/shard_map/pallas_call | solution.py:37
  411.9 7.2 %collective-permute-done.56 = f32[8,1152]{1,0:T(8,128)S(1)} collective-permute-done((f32[8,1152]{1,0:T(8,128)S(1)}, f32[8,1152]{1,0:T(8,128)S(1)}, u32[]{:S(2)}, u32[]{:S(2)}) %collective-permute-start.56) | collective-permute-done | bytes 36896 | tf_op jit(solution)/shard_map/ppermute | solution.py:549
  425.2 10.3 %collective-permute-done.58 = bf16[256,1280]{0,1:T(8,128)(2,1)S(1)} collective-permute-done((bf16[256,1280]{0,1:T(8,128)(2,1)}, bf16[256,1280]{0,1:T(8,128)(2,1)S(1)}, u32[]{:S(2)}, u32[]{:S(2)}) %collective-permute-start.58) | collective-permute-done | bytes 655392 | tf_op jit(solution)/shard_map/ppermute | solution.py:375
  453.9 11.4 %collective-permute-done.66 = bf16[64,2048]{0,1:T(8,128)(2,1)S(1)} collective-permute-done((bf16[64,2048]{0,1:T(8,128)(2,1)S(1)}, bf16[64,2048]{0,1:T(8,128)(2,1)S(1)}, u32[]{:S(2)}, u32[]{:S(2)}) %collective-permute-start.66) | collective-permute-done | bytes 262176 | tf_op jit(solution)/shard_map/ppermute | solution.py:375
  467.4 7.2 %collective-permute-done.71 = bf16[128,1280]{0,1:T(8,128)(2,1)S(1)} collective-permute-done((bf16[128,1280]{0,1:T(8,128)(2,1)S(1)}, bf16[128,1280]{0,1:T(8,128)(2,1)S(1)}, u32[]{:S(2)}, u32[]{:S(2)}) %collective-permute-start.71) | collective-permute-done | bytes 327712 | tf_op jit(solution)/shard_map/ppermute | solution.py:375
  489.9 9.7 %collective-permute-done.79 = f32[2,69,128]{2,1,0:T(8,128)S(1)} collective-permute-done((f32[2,69,128]{2,1,0:T(8,128)S(1)}, f32[2,69,128]{2,1,0:T(8,128)S(1)}, u32[]{:S(2)}, u32[]{:S(2)}) %collective-permute-start.79) | collective-permute-done | bytes 70688 | tf_op jit(solution)/shard_map/ppermute | solution.py:375
  499.6 5.5 collective-permute-done.75
  514.1 23.1 %collective-permute-done.80 = bf16[64,2048]{0,1:T(8,128)(2,1)S(1)} collective-permute-done((bf16[64,2048]{0,1:T(8,128)(2,1)S(1)}, bf16[64,2048]{0,1:T(8,128)(2,1)S(1)}, u32[]{:S(2)}, u32[]{:S(2)}) %collective-permute-start.80) | collective-permute-done | bytes 262176 | tf_op jit(solution)/shard_map/ppermute | solution.py:375
  541.8 14.5 %collective-permute-done.84 = f32[2,69,128]{2,1,0:T(8,128)S(1)} collective-permute-done((f32[2,69,128]{2,1,0:T(8,128)S(1)}, f32[2,69,128]{2,1,0:T(8,128)S(1)}, u32[]{:S(2)}, u32[]{:S(2)}) %collective-permute-start.84) | collective-permute-done | bytes 70688 | tf_op jit(solution)/shard_map/ppermute | solution.py:375
  (775 shorter events, 302.9 us)
Async XLA Ops:
  30.4 29.6 %collective-permute-start.7 = (bf16[256,1280]{1,0:T(8,128)(2,1)}, bf16[256,1280]{1,0:T(8,128)(2,1)}, u32[]{:S(2)}, u32[]{:S(2)}) collective-permute-start(bf16[256,1280]{1,0:T(8,128)(2,1)} %pad_maximum_fusion.7), channel_id=1, source_target_pairs={{0,16},{8,24},{16,0},{24,8},{1,17},{9,25},{17,1},{25,9},{2,18},{10... | collective-permute-start | bytes 1966088 | tf_op jit(solution)/shard_map/ppermute | solution.py:375
  31.9 29.7 %collective-permute-start.6 = (bf16[256,1280]{1,0:T(8,128)(2,1)}, bf16[256,1280]{1,0:T(8,128)(2,1)}, u32[]{:S(2)}, u32[]{:S(2)}) collective-permute-start(bf16[256,1280]{1,0:T(8,128)(2,1)} %pad_maximum_fusion.7), channel_id=1, source_target_pairs={{0,8},{8,0},{16,24},{24,16},{1,9},{9,1},{17,25},{25,17},{2,10},{10... | collective-permute-start | bytes 1966088 | tf_op jit(solution)/shard_map/ppermute | solution.py:375
  77.2 48.7 %collective-permute-start.16 = (bf16[256,2048]{1,0:T(8,128)(2,1)S(1)}, bf16[256,2048]{1,0:T(8,128)(2,1)S(1)}, u32[]{:S(2)}, u32[]{:S(2)}) collective-permute-start(bf16[256,2048]{1,0:T(8,128)(2,1)S(1)} %constant_dynamic-update-slice_fusion.7), channel_id=1, source_target_pairs={{0,16},{8,24},{16,0},{24,8},{1,17},{9,25},{17,1},{25,9},{2,18},{10... | collective-permute-start | bytes 3145736 | tf_op jit(solution)/shard_map/ppermute | solution.py:375
  79.8 41.9 %collective-permute-start.15 = (bf16[256,2048]{1,0:T(8,128)(2,1)S(1)}, bf16[256,2048]{1,0:T(8,128)(2,1)S(1)}, u32[]{:S(2)}, u32[]{:S(2)}) collective-permute-start(bf16[256,2048]{1,0:T(8,128)(2,1)S(1)} %constant_dynamic-update-slice_fusion.7), channel_id=1, source_target_pairs={{0,8},{8,0},{16,24},{24,16},{1,9},{9,1},{17,25},{25,17},{2,10},{10... | collective-permute-start | bytes 3145736 | tf_op jit(solution)/shard_map/ppermute | solution.py:375
  113.7 29.8 %collective-permute-start.12 = (f32[128,1024]{1,0:T(8,128)S(1)}, f32[128,1024]{1,0:T(8,128)S(1)}, u32[]{:S(2)}, u32[]{:S(2)}) collective-permute-start(f32[128,1024]{1,0:T(8,128)S(1)} %get-tuple-element.100), channel_id=1, source_target_pairs={{0,2},{4,6},{1,3},{5,7},{8,10},{12,14},{9,11},{13,15},{16,18},{20,... | collective-permute-start | bytes 1572872 | tf_op jit(solution)/shard_map/ppermute | solution.py:549
  121.2 32.7 %collective-permute-start.34 = (bf16[128,2048]{1,0:T(8,128)(2,1)}, bf16[128,2048]{1,0:T(8,128)(2,1)}, u32[]{:S(2)}, u32[]{:S(2)}) collective-permute-start(bf16[128,2048]{1,0:T(8,128)(2,1)} %pad_maximum_fusion.10), channel_id=1, source_target_pairs={{0,2},{2,0},{4,6},{6,4},{1,3},{3,1},{5,7},{7,5},{8,10},{10,8},{12,... | collective-permute-start | bytes 1572872 | tf_op jit(solution)/shard_map/ppermute | solution.py:375
  127.5 28.7 %collective-permute-start.27 = (bf16[256,1280]{1,0:T(8,128)(2,1)S(1)}, bf16[256,1280]{1,0:T(8,128)(2,1)S(1)}, u32[]{:S(2)}, u32[]{:S(2)}) collective-permute-start(bf16[256,1280]{1,0:T(8,128)(2,1)S(1)} %copy-done.86), channel_id=1, source_target_pairs={{0,16},{8,24},{16,0},{24,8},{1,17},{9,25},{17,1},{25,9},{2,18},{10... | collective-permute-start | bytes 1966088 | tf_op jit(solution)/shard_map/ppermute | solution.py:375
  161.1 42.2 %collective-permute-start.20 = (f32[512,1024]{1,0:T(8,128)S(1)}, f32[512,1024]{1,0:T(8,128)S(1)}, u32[]{:S(2)}, u32[]{:S(2)}) collective-permute-start(f32[512,1024]{1,0:T(8,128)S(1)} %fusion.27), channel_id=1, source_target_pairs={{0,1},{1,0},{2,3},{3,2},{4,5},{5,4},{6,7},{7,6},{8,9},{9,8},{10,11... | collective-permute-start | bytes 6291464 | tf_op jit(solution)/shard_map/ppermute | solution.py:375
  192.0 33.6 %collective-permute-start.38 = (bf16[128,2048]{1,0:T(8,128)(2,1)S(1)}, bf16[128,2048]{1,0:T(8,128)(2,1)S(1)}, u32[]{:S(2)}, u32[]{:S(2)}) collective-permute-start(bf16[128,2048]{1,0:T(8,128)(2,1)S(1)} %slice.836), channel_id=1, source_target_pairs={{0,8},{8,0},{16,24},{24,16},{1,9},{9,1},{17,25},{25,17},{2,10},{10... | collective-permute-start | bytes 1572872 | tf_op jit(solution)/shard_map/ppermute | solution.py:375
  280.2 37.3 %collective-permute-start.41 = (bf16[128,1024]{1,0:T(8,128)(2,1)}, bf16[128,1024]{1,0:T(8,128)(2,1)}, u32[]{:S(2)}, u32[]{:S(2)}) collective-permute-start(bf16[128,1024]{1,0:T(8,128)(2,1)} %get-tuple-element.296), channel_id=1, source_target_pairs={{0,0},{2,4},{4,2},{6,6},{1,1},{3,5},{5,3},{7,7},{8,8},{10,12},{12,... | collective-permute-start | bytes 786440 | tf_op jit(solution)/shard_map/ppermute | solution.py:520
  283.8 34.3 %collective-permute-start.42 = (bf16[128,1024]{1,0:T(8,128)(2,1)}, bf16[128,1024]{1,0:T(8,128)(2,1)}, u32[]{:S(2)}, u32[]{:S(2)}) collective-permute-start(bf16[128,1024]{1,0:T(8,128)(2,1)} %get-tuple-element.297), channel_id=1, source_target_pairs={{0,2},{2,6},{4,0},{6,4},{1,3},{3,7},{5,1},{7,5},{8,10},{10,14},{12... | collective-permute-start | bytes 786440 | tf_op jit(solution)/shard_map/ppermute | solution.py:521
  285.7 41.5 %collective-permute-start.47 = (bf16[128,2048]{0,1:T(8,128)(2,1)}, bf16[128,2048]{0,1:T(8,128)(2,1)}, u32[]{:S(2)}, u32[]{:S(2)}) collective-permute-start(bf16[128,2048]{0,1:T(8,128)(2,1)} %pad_maximum_fusion.12), channel_id=1, source_target_pairs={{0,16},{8,24},{16,0},{24,8},{1,17},{9,25},{17,1},{25,9},{2,18},{10... | collective-permute-start | bytes 1572872 | tf_op jit(solution)/shard_map/ppermute | solution.py:375
  286.9 40.2 %collective-permute-start.48 = (bf16[128,2048]{0,1:T(8,128)(2,1)}, bf16[128,2048]{0,1:T(8,128)(2,1)}, u32[]{:S(2)}, u32[]{:S(2)}) collective-permute-start(bf16[128,2048]{0,1:T(8,128)(2,1)} %pad_maximum_fusion.13), channel_id=1, source_target_pairs={{0,8},{8,0},{16,24},{24,16},{1,9},{9,1},{17,25},{25,17},{2,10},{10... | collective-permute-start | bytes 1572872 | tf_op jit(solution)/shard_map/ppermute | solution.py:375
  335.5 38.1 %collective-permute-start.52 = (bf16[256,2048]{0,1:T(8,128)(2,1)}, bf16[256,2048]{0,1:T(8,128)(2,1)}, u32[]{:S(2)}, u32[]{:S(2)}) collective-permute-start(bf16[256,2048]{0,1:T(8,128)(2,1)} %add_convert_fusion.3), channel_id=1, source_target_pairs={{0,16},{8,24},{16,0},{24,8},{1,17},{9,25},{17,1},{25,9},{2,18},{10... | collective-permute-start | bytes 3145736 | tf_op jit(solution)/shard_map/ppermute | solution.py:375
  339.0 34.6 %collective-permute-start.51 = (bf16[256,2048]{0,1:T(8,128)(2,1)}, bf16[256,2048]{0,1:T(8,128)(2,1)}, u32[]{:S(2)}, u32[]{:S(2)}) collective-permute-start(bf16[256,2048]{0,1:T(8,128)(2,1)} %add_convert_fusion.4), channel_id=1, source_target_pairs={{0,8},{8,0},{16,24},{24,16},{1,9},{9,1},{17,25},{25,17},{2,10},{10... | collective-permute-start | bytes 3145736 | tf_op jit(solution)/shard_map/ppermute | solution.py:375
  340.8 30.5 %collective-permute-start.54 = (bf16[128,1280]{0,1:T(8,128)(2,1)}, bf16[128,1280]{0,1:T(8,128)(2,1)}, u32[]{:S(2)}, u32[]{:S(2)}) collective-permute-start(bf16[128,1280]{0,1:T(8,128)(2,1)} %get-tuple-element.268), channel_id=1, source_target_pairs={{0,8},{8,0},{16,24},{24,16},{1,9},{9,1},{17,25},{25,17},{2,10},{10... | collective-permute-start | bytes 983048 | tf_op jit(solution)/shard_map/ppermute | solution.py:375
  342.0 30.6 %collective-permute-start.53 = (bf16[128,1280]{0,1:T(8,128)(2,1)}, bf16[128,1280]{0,1:T(8,128)(2,1)}, u32[]{:S(2)}, u32[]{:S(2)}) collective-permute-start(bf16[128,1280]{0,1:T(8,128)(2,1)} %get-tuple-element.269), channel_id=1, source_target_pairs={{0,16},{8,24},{16,0},{24,8},{1,17},{9,25},{17,1},{25,9},{2,18},{10... | collective-permute-start | bytes 983048 | tf_op jit(solution)/shard_map/ppermute | solution.py:375
  371.3 49.2 %collective-permute-start.60 = (bf16[128,2048]{0,1:T(8,128)(2,1)}, bf16[128,2048]{0,1:T(8,128)(2,1)}, u32[]{:S(2)}, u32[]{:S(2)}) collective-permute-start(bf16[128,2048]{0,1:T(8,128)(2,1)} %pad_maximum_fusion.14), channel_id=1, source_target_pairs={{0,16},{8,24},{16,0},{24,8},{1,17},{9,25},{17,1},{25,9},{2,18},{10... | collective-permute-start | bytes 1572872 | tf_op jit(solution)/shard_map/ppermute | solution.py:375
  372.6 48.0 %collective-permute-start.61 = (bf16[128,2048]{0,1:T(8,128)(2,1)}, bf16[128,2048]{0,1:T(8,128)(2,1)}, u32[]{:S(2)}, u32[]{:S(2)}) collective-permute-start(bf16[128,2048]{0,1:T(8,128)(2,1)} %pad_maximum_fusion.15), channel_id=1, source_target_pairs={{0,8},{8,0},{16,24},{24,16},{1,9},{9,1},{17,25},{25,17},{2,10},{10... | collective-permute-start | bytes 1572872 | tf_op jit(solution)/shard_map/ppermute | solution.py:375
  440.3 26.7 %collective-permute-start.67 = (bf16[128,1280]{0,1:T(8,128)(2,1)S(1)}, bf16[128,1280]{0,1:T(8,128)(2,1)S(1)}, u32[]{:S(2)}, u32[]{:S(2)}) collective-permute-start(bf16[128,1280]{0,1:T(8,128)(2,1)S(1)} %slice.1068), channel_id=1, source_target_pairs={{0,2},{2,0},{4,6},{6,4},{1,3},{3,1},{5,7},{7,5},{8,10},{10,8},{12,... | collective-permute-start | bytes 983048 | tf_op jit(solution)/shard_map/ppermute | solution.py:375
  443.4 38.1 %collective-permute-start.68 = (bf16[256,2048]{0,1:T(8,128)(2,1)S(1)}, bf16[256,2048]{0,1:T(8,128)(2,1)S(1)}, u32[]{:S(2)}, u32[]{:S(2)}) collective-permute-start(bf16[256,2048]{0,1:T(8,128)(2,1)S(1)} %add_convert_fusion.1), channel_id=1, source_target_pairs={{0,8},{8,0},{16,24},{24,16},{1,9},{9,1},{17,25},{25,17},{2,10},{10... | collective-permute-start | bytes 3145736 | tf_op jit(solution)/shard_map/ppermute | solution.py:375
  446.5 34.9 %collective-permute-start.69 = (bf16[256,2048]{0,1:T(8,128)(2,1)S(1)}, bf16[256,2048]{0,1:T(8,128)(2,1)S(1)}, u32[]{:S(2)}, u32[]{:S(2)}) collective-permute-start(bf16[256,2048]{0,1:T(8,128)(2,1)S(1)} %add_convert_fusion), channel_id=1, source_target_pairs={{0,16},{8,24},{16,0},{24,8},{1,17},{9,25},{17,1},{25,9},{2,18},{10... | collective-permute-start | bytes 3145736 | tf_op jit(solution)/shard_map/ppermute | solution.py:375
  508.6 28.5 %collective-permute-start.81 = (bf16[128,1280]{0,1:T(8,128)(2,1)S(1)}, bf16[128,1280]{0,1:T(8,128)(2,1)S(1)}, u32[]{:S(2)}, u32[]{:S(2)}) collective-permute-start(bf16[128,1280]{0,1:T(8,128)(2,1)S(1)} %slice.1066), channel_id=1, source_target_pairs={{0,2},{2,0},{4,6},{6,4},{1,3},{3,1},{5,7},{7,5},{8,10},{10,8},{12,... | collective-permute-start | bytes 983048 | tf_op jit(solution)/shard_map/ppermute | solution.py:375
  510.8 26.3 %collective-permute-start.80 = (bf16[64,2048]{0,1:T(8,128)(2,1)S(1)}, bf16[64,2048]{0,1:T(8,128)(2,1)S(1)}, u32[]{:S(2)}, u32[]{:S(2)}) collective-permute-start(bf16[64,2048]{0,1:T(8,128)(2,1)S(1)} %slice.1061), channel_id=1, source_target_pairs={{0,4},{2,6},{4,0},{6,2},{1,5},{3,7},{5,1},{7,3},{8,12},{10,14},{12... | collective-permute-start | bytes 786440 | tf_op jit(solution)/shard_map/ppermute | solution.py:375
  (211 other events, 2512.6 us)
